TPU v7x, 32 devices: a whole 2x2x4 slice. The times are simulated.
32 devices in a mesh: tm: 8 (over z, x), sensor: 4 (over y, core).
Axes of the slice: x: 2, y: 2, z: 4, core: 2. Of those that a mesh axis runs over, the one named last changes fastest.
Arguments:
- observations: bfloat16 [2048, 16384], P('tm', 'sensor'), may hold values from -6 to 6
- obs_list: int32 [2048, 64], P('tm', 'sensor'), may hold values from -1 to 127, as said below
- gain_rows: bfloat16 [16384, 1024], P('sensor'), may hold values from -0.0068359375 to 0.0068359375
- decay: float32 [2048, 1024], P('tm'), may hold values from 0 to 1
- smooth_gain: float32 [2048, 1024], P('tm'), may hold values from 0 to 1
- model_rate: float32 [1024], replicated, may hold values from 0.5 to 1
- first_state: float32 [1024], replicated, may hold values from -6 to 6
Outputs:
- filtered: float32 [2048, 1024], P('tm', 'sensor')
- smoothed: float32 [2048, 1024], P('tm', 'sensor')
Inputs may be any that keep to these rules, and one draw needn't show every extreme that they name: `obs_list`: in row t the 16 slots of sensor index j name distinct blocks from j * 32 to (j + 1) * 32 - 1; -1 marks an empty slot; slots of lower sensor indices are emptier.
All inputs are finite; a program needn't handle non-finite values.
Results may differ from a plain program's by a relative error of at most 0.0003.
Values sent between devices are 32-bit elements; how exact they have to be, the bound alone decides.
A program may use at most 64 MiB of HBM per device.

v0:
```python
import jax
import jax.numpy as jnp
from jax import lax
from jax.sharding import PartitionSpec as P


def prefix(part, axis, combine, identity, reverse):
    count = lax.axis_size(axis)
    place = lax.axis_index(axis)
    ahead = count - 1 - place if reverse else place
    gathered = jax.tree.map(lambda a: lax.all_gather(a, axis), part)
    state = jax.tree.map(lambda a, e: jnp.zeros_like(a) + jnp.asarray(e, a.dtype), part, identity)

    def one(hop, state):
        source = count - 1 - hop if reverse else hop
        return combine(
            state, jax.tree.map(lambda a: lax.dynamic_index_in_dim(a, source, 0, False), gathered)
        )

    return lax.fori_loop(0, ahead, one, state)


def link(earlier, later):
    return (later[0] * earlier[0], later[0] * earlier[1] + later[1])


def per_device(observations, obs_list, gain_rows, decay, smooth_gain, model_rate, first_state):
    sensor_count = lax.axis_size("sensor")
    sensor_index = lax.axis_index("sensor")
    time_index = lax.axis_index("tm")
    rows_here = observations.shape[0]
    block_count = observations.shape[1] // 128
    own_blocks = sensor_index * block_count + jnp.arange(block_count, dtype=jnp.int32)
    listed = jnp.any(obs_list[:, :, None] == own_blocks[None, None, :], axis=1).astype(jnp.float32)
    weighted = (
        (observations.reshape(rows_here, block_count, 128) * listed[:, :, None])
        .reshape(rows_here, block_count * 128)
        .astype(jnp.bfloat16)
    )
    partial_sum = jnp.dot(weighted, gain_rows, preferred_element_type=jnp.float32)
    width = gain_rows.shape[1] // sensor_count
    inflow = lax.psum_scatter(partial_sum, "sensor", scatter_dimension=1, tiled=True)
    start_col = sensor_index * width
    factors = lax.dynamic_slice_in_dim(decay, start_col, width, 1)
    gains = lax.dynamic_slice_in_dim(smooth_gain, start_col, width, 1)
    rates = lax.dynamic_slice_in_dim(model_rate, start_col, width, 0)
    initial = lax.dynamic_slice_in_dim(first_state, start_col, width, 0)
    identity = (jnp.ones((width,), jnp.float32), jnp.zeros((width,), jnp.float32))
    prod_fwd, local_fwd = lax.associative_scan(link, (factors, inflow), axis=0)
    carry_prod, carry_state = prefix((prod_fwd[-1], local_fwd[-1]), "tm", link, identity, False)
    entering = carry_prod * initial + carry_state
    filtered = local_fwd + prod_fwd * entering[None, :]
    hour_ids = time_index * rows_here + jnp.arange(rows_here, dtype=jnp.int32)
    total_hours = rows_here * lax.axis_size("tm")
    step_gain = jnp.where((hour_ids == total_hours - 1)[:, None], jnp.float32(0.0), gains)
    offset = filtered - step_gain * rates[None, :] * filtered
    prod_back, local_back = lax.associative_scan(link, (step_gain, offset), axis=0, reverse=True)
    _, after_state = prefix((prod_back[0], local_back[0]), "tm", link, identity, True)
    smoothed = local_back + prod_back * after_state[None, :]
    return (filtered, smoothed)


def solution(mesh):
    in_specs = (
        P("tm", "sensor"),
        P("tm", "sensor"),
        P("sensor", None),
        P("tm", None),
        P("tm", None),
        P(),
        P(),
    )
    out_specs = (P("tm", "sensor"), P("tm", "sensor"))
    return jax.shard_map(
        per_device, mesh=mesh, in_specs=in_specs, out_specs=out_specs, check_vma=False
    )
```

profile of v0, /device:TPU:0, one launch (start us, length us, event | category | flops | bytes accessed | tf_op | source)
XLA Modules:
  0.0 136.5 jit_solution(1999284869488464416)
XLA Ops:
  7.2 0.0 copy-start
  7.2 0.0 copy-start.2
  7.2 0.0 reduce-scatter.2.cloned.1.call-start
  7.3 1.0 compare_reduce_fusion
  8.3 0.1 copy.11
  8.4 1.1 mul.245
  9.5 0.0 copy-done.2
  9.5 8.7 %fusion.1 = f32[256,1024]{1,0:T(8,128)} fusion(bf16[4096,1024]{1,0:T(8,128)(2,1)} %param.13, f32[32,8,32,128]{3,2,1,0:T(8,128)S(1)} %bitcast.39, bf16[256,4096]{1,0:T(8,128)(2,1)S(1)} %copy-done.2), kind=kOutput, calls=%fused_computation.8 | convolution fusion | flops 2150629376 | bytes 15728640 | tf_op jit(solution)/shard_map/dot_general | solution.py:40
  18.2 0.0 reduce-scatter.2.cloned.1.call-update
  18.2 0.0 copy-done
  18.3 0.1 slice.496
  18.4 0.1 slice.500
  18.5 0.2 slice.495
  18.7 0.8 dynamic_slice.37
  19.5 26.4 %reduce-scatter.2.cloned.1.call-done = f32[256,256]{1,0:T(8,128)} async-done(((f32[256,1024]{1,0:T(8,128)}), f32[256,256]{1,0:T(8,128)}) %reduce-scatter.2.cloned.1.call-update) | async-done | bytes 262160 | tf_op jit(solution)/shard_map/reduce_scatter | solution.py:42
  46.0 1.0 slice.498
  47.0 1.0 slice.497
  48.0 0.0 copy-start.1
  48.4 0.0 slice-start
  50.0 0.0 copy-done.1
  50.0 0.2 slice.552
  50.2 0.1 fusion.4
  50.4 20.5 %all-gather = f32[8,1,256]{2,1,0:T(1,128)S(1)} all-gather(f32[1,1,256]{2,1,0:T(1,128)S(1)} %add_bitcast_fusion.3), channel_id=1, replica_groups=mesh['tm'=8,'sensor'=4] {'tm'}, dimensions={0}, use_global_device_ids=true | all-gather | bytes 9216 | tf_op jit(solution)/shard_map/all_gather | solution.py:11
  70.9 0.0 slice-done
  71.0 16.3 %all-gather.1 = f32[8,1,256]{2,1,0:T(1,128)S(1)} all-gather(f32[1,1,256]{2,1,0:T(1,128)S(1)} %add_bitcast_fusion.2), channel_id=1, replica_groups=mesh['tm'=8,'sensor'=4] {'tm'}, dimensions={0}, use_global_device_ids=true | all-gather | bytes 9216 | tf_op jit(solution)/shard_map/all_gather | solution.py:11
  87.3 0.8 multiply_add_fusion.18
  88.0 1.7 %multiply_subtract_fusion = (f32[256,256]{1,0:T(8,128)S(1)}, f32[256,256]{1,0:T(8,128)S(1)}, f32[256,256]{1,0:T(8,128)}) fusion(f32[256]{0:T(256)S(1)} %dynamic_slice.37, f32[256,1024]{1,0:T(8,128)} %param.15, s32[]{:T(128)S(6)} %select_n.24, pred[256]{0:T(512)(128)(4,1)S(1)} %add_compare_fusion, f32[256]{0:T(256)S(1)} %multiply_add_fusion.18, ...), kind=kLoop, calls=%fused_computation.10 | loop fusion | flops 524288 | bytes 2099460 | tf_op jit(solution)/shard_map/sub | solution.py:56
  89.8 0.1 slice.571
  89.9 0.1 slice.573
  90.0 0.1 slice.580
  90.1 0.1 slice.577
  90.2 0.1 slice.575
  90.3 0.1 slice.574
  90.4 0.1 slice.581
  90.5 0.1 slice.578
  90.6 0.1 slice.576
  91.7 0.1 slice.633
  91.8 0.1 slice.572
  92.0 0.1 slice.634
  93.0 0.1 add_multiply_fusion
  93.4 0.1 rev.8
  93.5 0.1 rev.9
  93.7 18.6 %all-gather.2 = f32[8,1,256]{2,1,0:T(1,128)S(1)} all-gather(f32[1,1,256]{2,1,0:T(1,128)S(1)} %add_bitcast_fusion.1), channel_id=1, replica_groups=mesh['tm'=8,'sensor'=4] {'tm'}, dimensions={0}, use_global_device_ids=true | all-gather | bytes 9216 | tf_op jit(solution)/shard_map/all_gather | solution.py:11
  112.3 16.3 %all-gather.3 = f32[8,1,256]{2,1,0:T(1,128)S(1)} all-gather(f32[1,1,256]{2,1,0:T(1,128)S(1)} %add_bitcast_fusion), channel_id=1, replica_groups=mesh['tm'=8,'sensor'=4] {'tm'}, dimensions={0}, use_global_device_ids=true | all-gather | bytes 9216 | tf_op jit(solution)/shard_map/all_gather | solution.py:11
  128.6 0.3 while.27
  128.9 0.7 multiply_add_fusion.2
  (261 shorter events, 3.5 us)
Async XLA Ops:
  7.2 11.1 %copy-start = (f32[256,1024]{1,0:T(8,128)S(1)}, f32[256,1024]{1,0:T(8,128)}, u32[]{:S(2)}) copy-start(f32[256,1024]{1,0:T(8,128)} %param.14) | copy-start | bytes 3145732
  7.2 2.3 %copy-start.2 = (bf16[256,4096]{1,0:T(8,128)(2,1)S(1)}, bf16[256,4096]{1,0:T(8,128)(2,1)}, u32[]{:S(2)}) copy-start(bf16[256,4096]{1,0:T(8,128)(2,1)} %param.11) | copy-start | bytes 6291460
  7.2 38.8 %reduce-scatter.2.cloned.1.call-start = ((), (), s32[]{:S(2)}) async-start(), calls=%async_computation.1 | async-start | bytes 1310720 | tf_op jit(solution)/shard_map/reduce_scatter | solution.py:42
  48.0 2.0 %copy-start.1 = (f32[256,256]{1,0:T(8,128)S(1)}, f32[256,256]{1,0:T(8,128)}, u32[]{:S(2)}) copy-start(f32[256,256]{1,0:T(8,128)} %reduce-scatter.2.cloned.1.call-done) | copy-start | bytes 786436
  48.4 22.5 %slice-start = ((f32[256,256]{1,0:T(8,128)}), f32[1,256]{1,0:T(1,128)S(1)}, s32[]{:S(2)}) async-start(f32[256,256]{1,0:T(8,128)} %reduce-scatter.2.cloned.1.call-done), calls=%async_computation.2 | async-start | bytes 2048 | tf_op jit(solution)/shard_map/slice | solution.py:49
Sparse Core Ops, SparseCore 0:
  18.4 27.5 reduce-scatter.1
where the time goes:
time: 137 us; the launch traced here: 136 us
  blocking collectives  71.6 us (52%)
  waiting for transfers between devices  26.5 us (19%)
  between operations  15.5 us (11%)
  matrix products  8.69 us (6%)
  local copies, waits for them, and re-layouts  8.52 us (6%)
  other arithmetic  5.41 us (4%)
    all_gather x4, blocking collectives, prefix(): gathered = jax.tree.map(lambda a: lax.all_gather(a, axis), part)  71.6 us
    reduce_scatter x1, waiting for transfers between devices, per_device(): lax.psum_scatter(partial_sum, 'sensor', scatter_dimension=1, tiled=True)  26.4 us
    dot_general x1, matrix products, per_device(): jnp.dot(weighted, gain_rows, preferred_element_type=jnp.float32)  8.69 us
    slice x53, local copies, waits for them, and re-layouts, per_device(): prod_fwd, local_fwd = lax.associative_scan(link, (factors, inflow), axis=0)  3.4 us
  transfers between devices with their start and end apart: 1, of which 1 were waited for; matrix products, arithmetic and copies ran while one was open for 1% of the time, Pallas kernels for 0%

commit v1 on v0

v1 whole, which is shorter than its diff:
```python
import functools
import jax
import jax.numpy as jnp
from jax import lax
from jax.experimental import pallas as pl
from jax.experimental.pallas import tpu as pltpu
from jax.sharding import PartitionSpec as P

LANES = 128
SEGS = 8
CHUNKS = 4
MESH = pl.DeviceIdType.MESH


def shift_rows(value, count, fill):
    rows = lax.broadcasted_iota(jnp.int32, value.shape, 0)
    moved = pltpu.roll(value, count % SEGS, 0)
    inside = (rows >= count) if count > 0 else (rows < SEGS + count)
    return jnp.where(inside, moved, jnp.float32(fill))


def factor_levels(factor, sign):
    levels = []
    for count in (1, 2, 4):
        levels.append(factor)
        factor = factor * shift_rows(factor, sign * count, 1.0)
    return levels, factor


def chain_rows(levels, value, sign):
    for level, count in zip(levels, (1, 2, 4)):
        value = value + level * shift_rows(value, sign * count, 0.0)
    return value


def kernel(
    nt, ny,
    obs, olist, gain, decay, sgain, rate, first,
    filt_out, smooth_out,
    obs_v, list_v, gain_v, dec_v, sg_v, rate_v, first_v,
    csend, crecv, acc, yrecv,
    fm, am, dm, gm, cm, pm, qm, bm,
    early, late, filt_v, smooth_v,
    obs_sem, gain0_sem, gain_sem, list_sem, dec_sem, sg_sem, par_sem,
    cs_sem, cr_sem, ys_sem, yr_sem, es_sem, er_sem, ls_sem, lr_sem, fo_sem, so_sem,
):
    tm = lax.axis_index("tm")
    sensor = lax.axis_index("sensor")
    y = sensor // 2
    core = sensor % 2
    partner = sensor + 1 - 2 * core
    hours, depth = obs_v.shape
    width = gain_v.shape[2]
    halves = width // LANES
    blocks = depth // LANES
    steps = hours // SEGS
    chunk = depth // CHUNKS

    def y_at(k):
        return lax.rem(y + k, ny)

    order = []
    for k in list(range(1, ny)) + [0]:
        order.append(y_at(k) * 2 + 1 - core)
        order.append(y_at(k) * 2 + core)

    def columns(dest):
        return pl.ds(pl.multiple_of(dest * width, LANES), width)

    list_copy = pltpu.make_async_copy(olist, list_v, list_sem)
    list_copy.start()
    obs_copies, gain0_copies = [], []
    for n in range(CHUNKS):
        part = pl.ds(n * chunk, chunk)
        obs_copies.append(pltpu.make_async_copy(obs.at[:, part], obs_v.at[:, part], obs_sem.at[n]))
        gain0_copies.append(
            pltpu.make_async_copy(
                gain.at[part, columns(order[0])], gain_v.at[0, part], gain0_sem.at[n]
            )
        )
        obs_copies[-1].start()
        gain0_copies[-1].start()
    gain_copies = []
    for b in range(1, 2 * ny):
        copy = pltpu.make_async_copy(gain.at[:, columns(order[b])], gain_v.at[b], gain_sem.at[b])
        copy.start()
        gain_copies.append(copy)
    dec_copies, sg_copies = [], []
    for j in range(halves):
        here = pl.ds(pl.multiple_of(sensor * width + j * LANES, LANES), LANES)
        dec_copies.append(pltpu.make_async_copy(decay.at[:, here], dec_v.at[j], dec_sem.at[j]))
        sg_copies.append(pltpu.make_async_copy(sgain.at[:, here], sg_v.at[j], sg_sem.at[j]))
        dec_copies[-1].start()
        sg_copies[-1].start()
    rate_copy = pltpu.make_async_copy(rate, rate_v, par_sem.at[0])
    first_copy = pltpu.make_async_copy(first, first_v, par_sem.at[1])
    rate_copy.start()
    first_copy.start()

    barrier = pltpu.get_barrier_semaphore()
    peers = [(tm, partner)]
    peers += [(tm, y_at(k) * 2 + core) for k in range(1, ny)]
    peers += [(lax.rem(tm + k, nt), sensor) for k in range(1, nt)]
    for peer in peers:
        pl.semaphore_signal(barrier, inc=1, device_id=peer, device_id_type=MESH)

    list_copy.wait()
    place = list_v[...] - sensor * blocks
    valid = (place >= 0) & (place < blocks)
    bit = jnp.where(valid, lax.shift_left(jnp.int32(1), jnp.where(valid, place, 0)), 0)
    bits = jnp.broadcast_to(jnp.sum(bit, axis=1, keepdims=True), (hours, LANES))

    def gate(b, carry):
        part = pl.ds(pl.multiple_of(b * LANES, LANES), LANES)
        listed = (bits & lax.shift_left(jnp.int32(1), b)) != 0
        value = obs_v[:, part].astype(jnp.float32)
        obs_v[:, part] = jnp.where(listed, value, 0.0).astype(jnp.bfloat16)
        return carry

    def put(ref, value):
        for j in range(halves):
            ref[j] = value[:, j * LANES:(j + 1) * LANES]

    total = None
    for n in range(CHUNKS):
        obs_copies[n].wait()
        lax.fori_loop(n * (blocks // CHUNKS), (n + 1) * (blocks // CHUNKS), gate, 0)
        gain0_copies[n].wait()
        part = pl.ds(n * chunk, chunk)
        term = jnp.dot(obs_v[:, part], gain_v[0, part], preferred_element_type=jnp.float32)
        total = term if total is None else total + term

    core_copies, y_copies = [], []
    for n, k in enumerate(list(range(1, ny)) + [0]):
        if n > 0:
            gain_copies[2 * n - 1].wait()
            total = jnp.dot(obs_v[...], gain_v[2 * n], preferred_element_type=jnp.float32)
        put(csend.at[n], total)
        if n == 0:
            pl.semaphore_wait(barrier, len(peers))
        copy = pltpu.make_async_remote_copy(
            csend.at[n], crecv.at[n], cs_sem.at[n], cr_sem.at[n],
            device_id=(tm, partner), device_id_type=MESH,
        )
        copy.start()
        core_copies.append(copy)
        gain_copies[2 * n].wait()
        put(acc.at[n], jnp.dot(obs_v[...], gain_v[2 * n + 1], preferred_element_type=jnp.float32))
        if k == 0:
            break
        copy.wait_recv()
        for j in range(halves):
            acc[n, j] = acc[n, j] + crecv[n, j]
            y_copy = pltpu.make_async_remote_copy(
                acc.at[n, j], yrecv.at[n, j], ys_sem.at[n, j], yr_sem.at[n, j],
                device_id=(tm, y_at(k) * 2 + core), device_id_type=MESH,
            )
            y_copy.start()
            y_copies.append(y_copy)

    rate_copy.wait()
    first_copy.wait()
    row_ids = lax.broadcasted_iota(jnp.int32, (SEGS, LANES), 0)
    last_row = (row_ids == SEGS - 1) & (tm == nt - 1)
    ones = jnp.ones((SEGS, LANES), jnp.float32)
    zeros = jnp.zeros((SEGS, LANES), jnp.float32)
    held = []
    for j in range(halves):
        dec_copies[j].wait()
        sg_copies[j].wait()
        rates = jnp.broadcast_to(rate_v[pl.ds(sensor * halves + j, 1), :], (SEGS, LANES))
        prod = ones
        for i in range(steps):
            d = dec_v[j, pl.ds(i, SEGS, stride=steps), :]
            prod = d * prod
            dm[j, i] = d
            pm[j, i] = prod
        back, linear = ones, zeros
        for i in reversed(range(steps)):
            g = sg_v[j, pl.ds(i, SEGS, stride=steps), :]
            if i == steps - 1:
                g = jnp.where(last_row, 0.0, g)
            c = 1.0 - g * rates
            linear = g * linear + c * pm[j, i]
            back = g * back
            gm[j, i] = g
            cm[j, i] = c
            bm[j, i] = linear
            qm[j, i] = back
        p_levels, p_all = factor_levels(prod, 1)
        q_levels, q_all = factor_levels(back, -1)
        p_before = shift_rows(p_all, 1, 1.0)
        q_after = shift_rows(q_all, -1, 1.0)
        b_all = chain_rows(q_levels, linear * p_before, -1)
        b_after = shift_rows(b_all, -1, 0.0)
        early[tm, j, 0:1] = p_all[SEGS - 1:SEGS]
        early[tm, j, 1:2] = q_all[0:1]
        early[tm, j, 2:3] = b_all[0:1]
        early[tm, j, 3:4] = jnp.zeros((1, LANES), jnp.float32)
        held.append((p_levels, q_levels, p_before, q_after, linear, b_after))
    early_copies = []
    for k in range(1, nt):
        copy = pltpu.make_async_remote_copy(
            early.at[tm], early.at[tm], es_sem.at[k], er_sem.at[k],
            device_id=(lax.rem(tm + k, nt), sensor), device_id_type=MESH,
        )
        copy.start()
        early_copies.append(copy)

    core_copies[-1].wait_recv()
    for j in range(halves):
        acc[ny - 1, j] = acc[ny - 1, j] + crecv[ny - 1, j]

    late_copies, carried = [], []
    for j in range(halves):
        for n in range(ny - 1):
            y_copies[n * halves + j].wait_recv()
        state = zeros
        for i in range(steps):
            rows = pl.ds(i, SEGS, stride=steps)
            inflow = acc[ny - 1, j, rows, :]
            for n in range(ny - 1):
                inflow = inflow + yrecv[n, j, rows, :]
            state = dm[j, i] * state + inflow
            fm[j, i] = state
        back = zeros
        for i in reversed(range(steps)):
            back = gm[j, i] * back + cm[j, i] * fm[j, i]
            am[j, i] = back
        p_levels, q_levels, p_before, q_after, linear, b_after = held[j]
        f_all = chain_rows(p_levels, state, 1)
        f_before = shift_rows(f_all, 1, 0.0)
        a_all = chain_rows(q_levels, back + linear * f_before, -1)
        a_after = shift_rows(a_all, -1, 0.0)
        late[j, tm, 0:1] = f_all[SEGS - 1:SEGS]
        late[j, tm, 1:2] = a_all[0:1]
        carried.append((f_before, a_after))
        for k in range(1, nt):
            copy = pltpu.make_async_remote_copy(
                late.at[j, tm], late.at[j, tm], ls_sem.at[j, k], lr_sem.at[j, k],
                device_id=(lax.rem(tm + k, nt), sensor), device_id_type=MESH,
            )
            copy.start()
            late_copies.append(copy)

    out_copies = []
    for j in range(halves):
        if j == 0:
            for copy in early_copies:
                copy.wait_recv()
        for k in range(1, nt):
            late_copies[j * (nt - 1) + k - 1].wait_recv()
        entry = first_v[pl.ds(sensor * halves + j, 1), :]
        entries, mine = [], entry
        for t in range(nt):
            mine = jnp.where(tm == t, entry, mine)
            entries.append(entry)
            entry = early[t, j, 0:1] * entry + late[j, t, 0:1]
        after = jnp.zeros((1, LANES), jnp.float32)
        mine_after = after
        for t in reversed(range(nt)):
            mine_after = jnp.where(tm == t, after, mine_after)
            after = early[t, j, 1:2] * after + (late[j, t, 1:2] + early[t, j, 2:3] * entries[t])
        _, _, p_before, q_after, _, b_after = held[j]
        f_before, a_after = carried[j]
        seg_entry = p_before * mine + f_before
        seg_after = q_after * mine_after + (a_after + b_after * mine)
        for i in range(steps):
            rows = pl.ds(i, SEGS, stride=steps)
            filt_v[j, rows, :] = fm[j, i] + pm[j, i] * seg_entry
            smooth_v[j, rows, :] = am[j, i] + bm[j, i] * seg_entry + qm[j, i] * seg_after
        here = pl.ds(j * LANES, LANES)
        for src, dst, sem in ((filt_v, filt_out, fo_sem), (smooth_v, smooth_out, so_sem)):
            copy = pltpu.make_async_copy(src.at[j], dst.at[:, here], sem.at[j])
            copy.start()
            out_copies.append(copy)

    for copy in core_copies + y_copies + early_copies + late_copies:
        copy.wait_send()
    for copy in out_copies:
        copy.wait()


def per_device(nt, ns, observations, obs_list, gain_rows, decay, smooth_gain, model_rate, first_state):
    ny = ns // 2
    hours, depth = observations.shape
    modes = gain_rows.shape[1]
    width = modes // ns
    halves = width // LANES
    steps = hours // SEGS
    f32 = jnp.float32
    dma = pltpu.SemaphoreType.DMA
    any_space = pl.BlockSpec(memory_space=pl.ANY)
    tiles = pltpu.VMEM((halves, steps, SEGS, LANES), f32)
    plane = pltpu.VMEM((halves, hours, LANES), f32)
    params = pltpu.VMEM((modes // LANES, LANES), f32)
    out = jax.ShapeDtypeStruct((hours, width), f32)
    return pl.pallas_call(
        functools.partial(kernel, nt, ny),
        out_shape=(out, out),
        in_specs=[any_space] * 7,
        out_specs=(any_space, any_space),
        scratch_shapes=[
            pltpu.VMEM((hours, depth), jnp.bfloat16),
            pltpu.VMEM(obs_list.shape, jnp.int32),
            pltpu.VMEM((ns, depth, width), jnp.bfloat16),
            plane, plane, params, params,
            pltpu.VMEM((ny, halves, hours, LANES), f32),
            pltpu.VMEM((ny, halves, hours, LANES), f32),
            pltpu.VMEM((ny, halves, hours, LANES), f32),
            pltpu.VMEM((max(ny - 1, 1), halves, hours, LANES), f32),
            tiles, tiles, tiles, tiles, tiles, tiles, tiles, tiles,
            pltpu.VMEM((nt, halves, 4, LANES), f32),
            pltpu.VMEM((halves, nt, 2, LANES), f32),
            plane, plane,
            dma((CHUNKS,)), dma((CHUNKS,)), dma((ns,)), dma, dma((halves,)), dma((halves,)), dma((2,)),
            dma((ny,)), dma((ny,)), dma((ny, halves)), dma((ny, halves)),
            dma((nt,)), dma((nt,)), dma((halves, nt)), dma((halves, nt)), dma((halves,)), dma((halves,)),
        ],
        compiler_params=pltpu.CompilerParams(
            collective_id=0, has_side_effects=True, vmem_limit_bytes=56 * 1024 * 1024
        ),
        cost_estimate=pl.CostEstimate(
            flops=2 * hours * depth * modes, bytes_accessed=2 * depth * (hours + modes), transcendentals=0
        ),
    )(
        observations, obs_list, gain_rows, decay, smooth_gain,
        model_rate.reshape(modes // LANES, LANES), first_state.reshape(modes // LANES, LANES),
    )


def solution(mesh):
    nt, ns = mesh.shape["tm"], mesh.shape["sensor"]
    in_specs = (
        P("tm", "sensor"),
        P("tm", "sensor"),
        P("sensor", None),
        P("tm", None),
        P("tm", None),
        P(),
        P(),
    )
    out_specs = (P("tm", "sensor"), P("tm", "sensor"))
    return jax.shard_map(
        functools.partial(per_device, nt, ns),
        mesh=mesh, in_specs=in_specs, out_specs=out_specs, check_vma=False,
    )
```

time: 137 us -> 30.7 us (0.22)
  blocking collectives: 71.6 us -> 0 us
  waiting for transfers between devices: 26.5 us -> 0 us
  Pallas kernels: 0 us -> 25 us
  between operations: 15.5 us -> 0.64 us
  matrix products: 8.69 us -> 0 us
  other arithmetic: 5.41 us -> 0 us
  local copies, waits for them, and re-layouts: 8.52 us -> 4.81 us
    all_gather x4 -> x0, blocking collectives: 71.6 us -> none  [prefix(): gathered = jax.tree.map(lambda a: lax.all_gather(a, axis), part)]
    reduce_scatter x1 -> x0, waiting for transfers between devices: 26.4 us -> none  [per_device(): lax.psum_scatter(partial_sum, 'sensor', scatter_dimension=1, tiled=True)]
    pallas_call x0 -> x1, Pallas kernels: none -> 25 us  [per_device(): pl.pallas_call(functools.partial(kernel, nt, ny), out_shape=(out, out), i...]
    dot_general x1 -> x0, matrix products: 8.69 us -> none  [per_device(): jnp.dot(weighted, gain_rows, preferred_element_type=jnp.float32)]
    slice x111 -> x0, local copies, waits for them, and re-layouts: 5.29 us -> none  [the longest x53 3.4 us: per_device(): prod_fwd, local_fwd = lax.associative_scan(link, (factors, inflow), axis=0)]
    unnamed x10 -> x3, local copies, waits for them, and re-layouts: 0.02 us -> 4.81 us
    add x53 -> x0, other arithmetic: 2.13 us -> none  [the longest x1 0.76 us: per_device(): entering = carry_prod * initial + carry_state]
    sub x1 -> x0, other arithmetic: 1.71 us -> none  [per_device(): offset = filtered - step_gain * rates[None, :] * filtered]
  transfers between devices with their start and end apart: 1 -> 0, of which waited for: 1 -> 0; matrix products, arithmetic and copies ran while one was open for 1% -> 0% of each run, Pallas kernels for 0% -> 0%
where the time goes in v1:
time: 30.7 us; the launch traced here: 30.4 us
  Pallas kernels  25 us (81%)
  local copies, waits for them, and re-layouts  4.81 us (16%)
  between operations  0.64 us (2%)
    pallas_call x1, Pallas kernels, per_device(): pl.pallas_call(functools.partial(kernel, nt, ny), out_shape=(out, out), i...  25 us
    unnamed x3, local copies, waits for them, and re-layouts  4.81 us

profile of v1, /device:TPU:0, one launch (start us, length us, event | category | flops | bytes accessed | tf_op | source)
XLA Modules:
  0.0 30.4 jit_solution(9898751399400857888)
XLA Ops:
  0.6 1.5 %copy.9.olist = s32[256,16]{1,0:T(8,128)} copy(s32[256,16]{0,1:T(8,128)} %param.8) | data formatting | bytes 32768 | tf_op args[1]
  2.1 25.0 %shard_map.86 = (f32[256,256]{1,0:T(8,128)}, f32[256,256]{1,0:T(8,128)}) custom-call(bf16[256,4096]{1,0:T(8,128)(2,1)} %obs.1, s32[256,16]{1,0:T(8,128)} %copy.9.olist, bf16[4096,1024]{1,0:T(8,128)(2,1)} %gain.1, f32[256,1024]{1,0:T(8,128)} %decay.1, f32[256,1024]{1,0:T(8,128)} %sgain.1, f32[8,128]{1,0:T(8,128)} %bitcast.2, f32[8,128]{1,0:T(8,128)} %bitcast.3), custom_call_target="tpu_custom_call" | custom-call | flops 2147483648 | bytes 10485760 | tf_op jit(solution)/shard_map/pallas_call | solution.py:298
  27.1 1.7 %copy.12 = f32[256,256]{1,0:T(8,128)} copy(f32[256,256]{1,0:T(8,128)} %get-tuple-element.4) | data formatting | bytes 524288
  28.8 1.7 %copy.13 = f32[256,256]{1,0:T(8,128)} copy(f32[256,256]{1,0:T(8,128)} %get-tuple-element.5) | data formatting | bytes 524288

commit v2 on v1

--- a/solution.py
+++ b/solution.py
@@ -42,7 +42,7 @@
     fm, am, dm, gm, cm, pm, qm, bm,
     early, late, filt_v, smooth_v,
     obs_sem, gain0_sem, gain_sem, list_sem, dec_sem, sg_sem, par_sem,
-    cs_sem, cr_sem, ys_sem, yr_sem, es_sem, er_sem, ls_sem, lr_sem, fo_sem, so_sem,
+    cs_sem, cr_sem, ys_sem, yr_sem, es_sem, er_sem, ls_sem, lr_sem,
 ):
     tm = lax.axis_index("tm")
     sensor = lax.axis_index("sensor")
@@ -82,21 +82,16 @@
         gain0_copies[-1].start()
     gain_copies = []
     for b in range(1, 2 * ny):
-        copy = pltpu.make_async_copy(gain.at[:, columns(order[b])], gain_v.at[b], gain_sem.at[b])
-        copy.start()
-        gain_copies.append(copy)
+        gain_copies.append(
+            pltpu.make_async_copy(gain.at[:, columns(order[b])], gain_v.at[b], gain_sem.at[b])
+        )
     dec_copies, sg_copies = [], []
     for j in range(halves):
         here = pl.ds(pl.multiple_of(sensor * width + j * LANES, LANES), LANES)
         dec_copies.append(pltpu.make_async_copy(decay.at[:, here], dec_v.at[j], dec_sem.at[j]))
         sg_copies.append(pltpu.make_async_copy(sgain.at[:, here], sg_v.at[j], sg_sem.at[j]))
-        dec_copies[-1].start()
-        sg_copies[-1].start()
     rate_copy = pltpu.make_async_copy(rate, rate_v, par_sem.at[0])
     first_copy = pltpu.make_async_copy(first, first_v, par_sem.at[1])
-    rate_copy.start()
-    first_copy.start()
-
     barrier = pltpu.get_barrier_semaphore()
     peers = [(tm, partner)]
     peers += [(tm, y_at(k) * 2 + core) for k in range(1, ny)]
@@ -108,7 +103,8 @@
     place = list_v[...] - sensor * blocks
     valid = (place >= 0) & (place < blocks)
     bit = jnp.where(valid, lax.shift_left(jnp.int32(1), jnp.where(valid, place, 0)), 0)
-    bits = jnp.broadcast_to(jnp.sum(bit, axis=1, keepdims=True), (hours, LANES))
+    flat = jnp.broadcast_to(jnp.sum(bit, axis=0, keepdims=True), (LANES, hours))
+    bits = jnp.transpose(flat)
 
     def gate(b, carry):
         part = pl.ds(pl.multiple_of(b * LANES, LANES), LANES)
@@ -126,9 +122,14 @@
         obs_copies[n].wait()
         lax.fori_loop(n * (blocks // CHUNKS), (n + 1) * (blocks // CHUNKS), gate, 0)
         gain0_copies[n].wait()
+        if n == CHUNKS // 2 - 1:
+            gain_copies[0].start()
         part = pl.ds(n * chunk, chunk)
         term = jnp.dot(obs_v[:, part], gain_v[0, part], preferred_element_type=jnp.float32)
         total = term if total is None else total + term
+
+    for copy in gain_copies[1:] + dec_copies + sg_copies + [rate_copy, first_copy]:
+        copy.start()
 
     core_copies, y_copies = [], []
     for n, k in enumerate(list(range(1, ny)) + [0]):
@@ -138,18 +139,19 @@
         put(csend.at[n], total)
         if n == 0:
             pl.semaphore_wait(barrier, len(peers))
-        copy = pltpu.make_async_remote_copy(
-            csend.at[n], crecv.at[n], cs_sem.at[n], cr_sem.at[n],
-            device_id=(tm, partner), device_id_type=MESH,
-        )
-        copy.start()
-        core_copies.append(copy)
+        for j in range(halves):
+            copy = pltpu.make_async_remote_copy(
+                csend.at[n, j], crecv.at[n, j], cs_sem.at[n, j], cr_sem.at[n, j],
+                device_id=(tm, partner), device_id_type=MESH,
+            )
+            copy.start()
+            core_copies.append(copy)
         gain_copies[2 * n].wait()
         put(acc.at[n], jnp.dot(obs_v[...], gain_v[2 * n + 1], preferred_element_type=jnp.float32))
         if k == 0:
             break
-        copy.wait_recv()
         for j in range(halves):
+            core_copies[n * halves + j].wait_recv()
             acc[n, j] = acc[n, j] + crecv[n, j]
             y_copy = pltpu.make_async_remote_copy(
                 acc.at[n, j], yrecv.at[n, j], ys_sem.at[n, j], yr_sem.at[n, j],
@@ -207,8 +209,8 @@
         copy.start()
         early_copies.append(copy)
 
-    core_copies[-1].wait_recv()
-    for j in range(halves):
+    for j in range(halves):
+        core_copies[(ny - 1) * halves + j].wait_recv()
         acc[ny - 1, j] = acc[ny - 1, j] + crecv[ny - 1, j]
 
     late_copies, carried = [], []
@@ -243,7 +245,6 @@
             copy.start()
             late_copies.append(copy)
 
-    out_copies = []
     for j in range(halves):
         if j == 0:
             for copy in early_copies:
@@ -269,16 +270,11 @@
             rows = pl.ds(i, SEGS, stride=steps)
             filt_v[j, rows, :] = fm[j, i] + pm[j, i] * seg_entry
             smooth_v[j, rows, :] = am[j, i] + bm[j, i] * seg_entry + qm[j, i] * seg_after
-        here = pl.ds(j * LANES, LANES)
-        for src, dst, sem in ((filt_v, filt_out, fo_sem), (smooth_v, smooth_out, so_sem)):
-            copy = pltpu.make_async_copy(src.at[j], dst.at[:, here], sem.at[j])
-            copy.start()
-            out_copies.append(copy)
+        filt_out[:, j * LANES:(j + 1) * LANES] = filt_v[j]
+        smooth_out[:, j * LANES:(j + 1) * LANES] = smooth_v[j]
 
     for copy in core_copies + y_copies + early_copies + late_copies:
         copy.wait_send()
-    for copy in out_copies:
-        copy.wait()
 
 
 def per_device(nt, ns, observations, obs_list, gain_rows, decay, smooth_gain, model_rate, first_state):
@@ -294,15 +290,16 @@
     tiles = pltpu.VMEM((halves, steps, SEGS, LANES), f32)
     plane = pltpu.VMEM((halves, hours, LANES), f32)
     params = pltpu.VMEM((modes // LANES, LANES), f32)
-    out = jax.ShapeDtypeStruct((hours, width), f32)
+    out = pltpu.VMEM((hours, width), f32)
+    vmem_space = pl.BlockSpec(memory_space=pltpu.VMEM)
     return pl.pallas_call(
         functools.partial(kernel, nt, ny),
         out_shape=(out, out),
         in_specs=[any_space] * 7,
-        out_specs=(any_space, any_space),
+        out_specs=(vmem_space, vmem_space),
         scratch_shapes=[
             pltpu.VMEM((hours, depth), jnp.bfloat16),
-            pltpu.VMEM(obs_list.shape, jnp.int32),
+            pltpu.VMEM(obs_list.shape[::-1], jnp.int32),
             pltpu.VMEM((ns, depth, width), jnp.bfloat16),
             plane, plane, params, params,
             pltpu.VMEM((ny, halves, hours, LANES), f32),
@@ -314,8 +311,8 @@
             pltpu.VMEM((halves, nt, 2, LANES), f32),
             plane, plane,
             dma((CHUNKS,)), dma((CHUNKS,)), dma((ns,)), dma, dma((halves,)), dma((halves,)), dma((2,)),
-            dma((ny,)), dma((ny,)), dma((ny, halves)), dma((ny, halves)),
-            dma((nt,)), dma((nt,)), dma((halves, nt)), dma((halves, nt)), dma((halves,)), dma((halves,)),
+            dma((ny, halves)), dma((ny, halves)), dma((ny, halves)), dma((ny, halves)),
+            dma((nt,)), dma((nt,)), dma((halves, nt)), dma((halves, nt)),
         ],
         compiler_params=pltpu.CompilerParams(
             collective_id=0, has_side_effects=True, vmem_limit_bytes=56 * 1024 * 1024
@@ -324,7 +321,7 @@
             flops=2 * hours * depth * modes, bytes_accessed=2 * depth * (hours + modes), transcendentals=0
         ),
     )(
-        observations, obs_list, gain_rows, decay, smooth_gain,
+        observations, obs_list.T, gain_rows, decay, smooth_gain,
         model_rate.reshape(modes // LANES, LANES), first_state.reshape(modes // LANES, LANES),
     )
 

time: 30.7 us -> 24.5 us (0.80)
  local copies, waits for them, and re-layouts: 4.81 us -> 1.41 us
  Pallas kernels: 25 us -> 22.3 us
    unnamed x3 -> x2, local copies, waits for them, and re-layouts: 4.81 us -> 1.41 us
    pallas_call x1, Pallas kernels: 25 us -> 22.3 us  [per_device(): pl.pallas_call(functools.partial(kernel, nt, ny), out_shape=(out, out), i...]
where the time goes in v2:
time: 24.5 us; the launch traced here: 24.3 us
  Pallas kernels  22.3 us (91%)
  local copies, waits for them, and re-layouts  1.41 us (6%)
  between operations  0.64 us (3%)
    pallas_call x1, Pallas kernels, per_device(): pl.pallas_call(functools.partial(kernel, nt, ny), out_shape=(out, out), i...  22.3 us
    unnamed x2, local copies, waits for them, and re-layouts  1.41 us

profile of v2, /device:TPU:0, one launch (start us, length us, event | category | flops | bytes accessed | tf_op | source)
XLA Modules:
  0.0 24.3 jit_solution(4355976191628378727)
XLA Ops:
  0.6 22.3 %shard_map.86 = (f32[256,256]{1,0:T(8,128)S(1)}, f32[256,256]{1,0:T(8,128)S(1)}) custom-call(bf16[256,4096]{1,0:T(8,128)(2,1)} %obs.1, s32[16,256]{1,0:T(8,128)} %bitcast.3, bf16[4096,1024]{1,0:T(8,128)(2,1)} %gain.1, f32[256,1024]{1,0:T(8,128)} %decay.1, f32[256,1024]{1,0:T(8,128)} %sgain.1, f32[8,128]{1,0:T(8,128)} %bitcast.4, f32[8,128]{1,0:T(8,128)} %bitcast.5), custom_call_target="tpu_custom_call" | custom-call | flops 2147483648 | bytes 10485760 | tf_op jit(solution)/shard_map/pallas_call | solution.py:295
  22.9 0.7 %copy.11 = f32[256,256]{1,0:T(8,128)} copy(f32[256,256]{1,0:T(8,128)S(1)} %get-tuple-element.2) | data formatting | bytes 524288
  23.6 0.7 %copy.12 = f32[256,256]{1,0:T(8,128)} copy(f32[256,256]{1,0:T(8,128)S(1)} %get-tuple-element.3) | data formatting | bytes 524288

commit v3 on v2

v3 whole, which is shorter than its diff:
```python
import functools
import jax
import jax.numpy as jnp
from jax import lax
from jax.experimental import pallas as pl
from jax.experimental.pallas import tpu as pltpu
from jax.sharding import PartitionSpec as P

LANES = 128
SEGS = 8
CHUNKS = 4
MESH = pl.DeviceIdType.MESH


def shift_rows(value, count, fill):
    rows = lax.broadcasted_iota(jnp.int32, value.shape, 0)
    moved = pltpu.roll(value, count % SEGS, 0)
    inside = (rows >= count) if count > 0 else (rows < SEGS + count)
    return jnp.where(inside, moved, jnp.float32(fill))


def factor_levels(factor, sign):
    levels = []
    for count in (1, 2, 4):
        levels.append(factor)
        factor = factor * shift_rows(factor, sign * count, 1.0)
    return levels, factor


def chain_rows(levels, value, sign):
    for level, count in zip(levels, (1, 2, 4)):
        value = value + level * shift_rows(value, sign * count, 0.0)
    return value


def kernel(
    nt, ny,
    obs, olist, gain, decay, sgain, rate, first,
    filt_out, smooth_out,
    obs_v, list_v, gain_v, dec_v, sg_v, rate_v, first_v,
    csend, crecv, acc, yrecv,
    um, fm, am, dm, gm, cm, pm, qm,
    early, late, part_send, part_recv, filt_v, smooth_v,
    obs_sem, gain0_sem, gain_sem, list_sem, dec_sem, sg_sem, par_sem,
    cs_sem, cr_sem, ys_sem, yr_sem, ps_sem, pr_sem, es_sem, er_sem, ls_sem, lr_sem,
):
    tm = lax.axis_index("tm")
    sensor = lax.axis_index("sensor")
    y = sensor // 2
    core = sensor % 2
    partner = sensor + 1 - 2 * core
    hours, depth = obs_v.shape
    halves = acc.shape[1]
    width = halves * LANES
    blocks = depth // LANES
    steps = hours // SEGS
    chunk = depth // CHUNKS
    shifts = list(range(1, ny)) + [0]
    last = ny - 1

    def mine_at(k):
        return lax.rem(y + k, ny) * 2 + core

    def columns(dest, j):
        return pl.ds(pl.multiple_of(dest * width + j * LANES, LANES), LANES)

    def gain_pair(n, j, rows, sems):
        own = mine_at(shifts[n])
        other = own + 1 - 2 * core
        slot = gain_v.at[n * halves + j]
        return [
            pltpu.make_async_copy(
                gain.at[rows, columns(dest, j)], slot.at[rows, pl.ds(side * LANES, LANES)], sems.at[side]
            )
            for side, dest in enumerate((other, own))
        ]

    list_copy = pltpu.make_async_copy(olist, list_v, list_sem)
    list_copy.start()
    obs_copies, gain0_copies = [], []
    for n in range(CHUNKS):
        part = pl.ds(n * chunk, chunk)
        obs_copies.append(pltpu.make_async_copy(obs.at[:, part], obs_v.at[:, part], obs_sem.at[n]))
        gain0_copies.append(gain_pair(0, 0, part, gain0_sem.at[n]))
        for copy in [obs_copies[-1]] + gain0_copies[-1]:
            copy.start()
    everything = pl.ds(0, depth)
    gain_copies = {
        (n, j): gain_pair(n, j, everything, gain_sem.at[n * halves + j])
        for n in range(ny) for j in range(halves) if n + j > 0
    }
    pairs = list(gain_copies)
    steady_copies = []
    for n in range(ny):
        for j in range(halves):
            here = columns(mine_at(shifts[n]), j)
            steady_copies.append(pltpu.make_async_copy(decay.at[:, here], dec_v.at[n, j], dec_sem.at[n, j]))
            steady_copies.append(pltpu.make_async_copy(sgain.at[:, here], sg_v.at[n, j], sg_sem.at[n, j]))
    steady_copies.append(pltpu.make_async_copy(rate, rate_v, par_sem.at[0]))
    steady_copies.append(pltpu.make_async_copy(first, first_v, par_sem.at[1]))

    barrier = pltpu.get_barrier_semaphore()
    peers = [(tm, partner)]
    peers += [(tm, mine_at(k)) for k in range(1, ny)]
    peers += [(lax.rem(tm + k, nt), sensor) for k in range(1, nt)]
    for peer in peers:
        pl.semaphore_signal(barrier, inc=1, device_id=peer, device_id_type=MESH)

    list_copy.wait()
    place = list_v[...] - sensor * blocks
    valid = (place >= 0) & (place < blocks)
    bit = jnp.where(valid, lax.shift_left(jnp.int32(1), jnp.where(valid, place, 0)), 0)
    flat = jnp.broadcast_to(jnp.sum(bit, axis=0, keepdims=True), (LANES, hours))
    bits = jnp.transpose(flat)

    def gate(b, carry):
        part = pl.ds(pl.multiple_of(b * LANES, LANES), LANES)
        listed = (bits & lax.shift_left(jnp.int32(1), b)) != 0
        value = obs_v[:, part].astype(jnp.float32)
        obs_v[:, part] = jnp.where(listed, value, 0.0).astype(jnp.bfloat16)
        return carry

    total = None
    for n in range(CHUNKS):
        obs_copies[n].wait()
        lax.fori_loop(n * (blocks // CHUNKS), (n + 1) * (blocks // CHUNKS), gate, 0)
        for copy in gain0_copies[n]:
            copy.wait()
        if n == CHUNKS // 2 - 1:
            for copy in gain_copies[pairs[0]]:
                copy.start()
        part = pl.ds(n * chunk, chunk)
        term = jnp.dot(obs_v[:, part], gain_v[0, part], preferred_element_type=jnp.float32)
        total = term if total is None else total + term
    for copy in steady_copies:
        copy.start()
    for pair in pairs[1:]:
        for copy in gain_copies[pair]:
            copy.start()

    core_copies, y_copies = {}, {}

    def hand_over(n, j, total):
        csend[n, j] = total[:, :LANES]
        copy = pltpu.make_async_remote_copy(
            csend.at[n, j], crecv.at[n, j], cs_sem.at[n, j], cr_sem.at[n, j],
            device_id=(tm, partner), device_id_type=MESH,
        )
        copy.start()
        core_copies[n, j] = copy
        acc[n, j] = total[:, LANES:]

    def product(n, j):
        for copy in gain_copies[n, j]:
            copy.wait()
        hand_over(
            n, j, jnp.dot(obs_v[...], gain_v[n * halves + j], preferred_element_type=jnp.float32)
        )

    def join(n, j):
        core_copies[n, j].wait_recv()
        acc[n, j] = acc[n, j] + crecv[n, j]

    def send_y(n, j):
        join(n, j)
        copy = pltpu.make_async_remote_copy(
            acc.at[n, j], yrecv.at[n, j], ys_sem.at[n, j], yr_sem.at[n, j],
            device_id=(tm, mine_at(shifts[n])), device_id_type=MESH,
        )
        copy.start()
        y_copies[n, j] = copy

    away = [(n, j) for n in range(last) for j in range(halves)]
    home = [(last, j) for j in range(halves)]
    pl.semaphore_wait(barrier, len(peers))
    hand_over(0, 0, total)
    if away:
        send_y(0, 0)
    for n, j in away[1:]:
        product(n, j)

    for copy in steady_copies:
        copy.wait()
    row_ids = lax.broadcasted_iota(jnp.int32, (SEGS, LANES), 0)
    last_row = (row_ids == SEGS - 1) & (tm == nt - 1)
    ones = jnp.ones((SEGS, LANES), jnp.float32)
    zeros = jnp.zeros((SEGS, LANES), jnp.float32)
    rates = {
        (n, j): jnp.broadcast_to(rate_v[pl.ds(mine_at(shifts[n]) * halves + j, 1), :], (SEGS, LANES))
        for n, j in away + home
    }
    prod = {at: ones for at in away + home}
    for i in range(steps):
        for at in away + home:
            d = dec_v[at[0], at[1], pl.ds(i, SEGS, stride=steps), :]
            prod[at] = d * prod[at]
            dm[at[0], at[1], i] = d
            pm[at[0], at[1], i] = prod[at]
    back = {at: ones for at in away + home}
    linear = {at: zeros for at in away + home}
    for i in reversed(range(steps)):
        for at in away + home:
            n, j = at
            g = sg_v[n, j, pl.ds(i, SEGS, stride=steps), :]
            if i == steps - 1:
                g = jnp.where(last_row, 0.0, g)
            c = 1.0 - g * rates[at]
            linear[at] = g * linear[at] + c * pm[n, j, i]
            back[at] = g * back[at]
            gm[n, j, i] = g
            cm[n, j, i] = c
            if n == last:
                qm[j, i] = back[at]
    p_levels, q_levels, p_before, q_after = {}, {}, {}, {}
    for at in away + home:
        p_levels[at], p_all = factor_levels(prod[at], 1)
        q_levels[at], q_all = factor_levels(back[at], -1)
        p_before[at] = shift_rows(p_all, 1, 1.0)
        q_after[at] = shift_rows(q_all, -1, 1.0)
        if at[0] == last:
            b_all = chain_rows(q_levels[at], linear[at] * p_before[at], -1)
            early[tm, at[1], 0:1] = p_all[SEGS - 1:SEGS]
            early[tm, at[1], 1:2] = q_all[0:1]
            early[tm, at[1], 2:3] = b_all[0:1]
            early[tm, at[1], 3:4] = jnp.zeros((1, LANES), jnp.float32)
    for at in away[1:]:
        send_y(*at)

    def summaries(group):
        state = {at: zeros for at in group}
        for i in range(steps):
            for at in group:
                n, j = at
                inflow = acc[n, j, pl.ds(i, SEGS, stride=steps), :]
                if n == last:
                    um[j, i] = inflow
                state[at] = dm[n, j, i] * state[at] + inflow
                fm[n, j, i] = state[at]
        back = {at: zeros for at in group}
        for i in reversed(range(steps)):
            for at in group:
                n, j = at
                back[at] = gm[n, j, i] * back[at] + cm[n, j, i] * fm[n, j, i]
        result = {}
        for at in group:
            f_all = chain_rows(p_levels[at], state[at], 1)
            f_before = shift_rows(f_all, 1, 0.0)
            a_all = chain_rows(q_levels[at], back[at] + linear[at] * f_before, -1)
            result[at] = (f_all[SEGS - 1:SEGS], a_all[0:1])
        return result

    part_copies = []
    away_result = summaries(away)
    for n in range(last):
        for j in range(halves):
            part_send[n, j, 0:1], part_send[n, j, 1:2] = away_result[n, j]
        copy = pltpu.make_async_remote_copy(
            part_send.at[n], part_recv.at[n], ps_sem.at[n], pr_sem.at[n],
            device_id=(tm, mine_at(shifts[n])), device_id_type=MESH,
        )
        copy.start()
        part_copies.append(copy)
    early_copies = []
    for k in range(1, nt):
        copy = pltpu.make_async_remote_copy(
            early.at[tm], early.at[tm], es_sem.at[k], er_sem.at[k],
            device_id=(lax.rem(tm + k, nt), sensor), device_id_type=MESH,
        )
        copy.start()
        early_copies.append(copy)

    for at in home:
        if at != (0, 0):
            product(*at)
    for at in home:
        join(*at)
    home_result = summaries(home)
    for copy in part_copies:
        copy.wait_recv()
    for n, j in home:
        f_row, a_row = home_result[n, j]
        for source in range(last):
            f_row = f_row + part_recv[source, j, 0:1]
            a_row = a_row + part_recv[source, j, 1:2]
        late[tm, j, 0:1] = f_row
        late[tm, j, 1:2] = a_row
    late_copies = []
    for k in range(1, nt):
        copy = pltpu.make_async_remote_copy(
            late.at[tm], late.at[tm], ls_sem.at[k], lr_sem.at[k],
            device_id=(lax.rem(tm + k, nt), sensor), device_id_type=MESH,
        )
        copy.start()
        late_copies.append(copy)
    for copy in early_copies + late_copies:
        copy.wait_recv()

    bounds = []
    for j in range(halves):
        entry = first_v[pl.ds(sensor * halves + j, 1), :]
        entries, mine = [], entry
        for t in range(nt):
            mine = jnp.where(tm == t, entry, mine)
            entries.append(entry)
            entry = early[t, j, 0:1] * entry + late[t, j, 0:1]
        after = jnp.zeros((1, LANES), jnp.float32)
        mine_after = after
        for t in reversed(range(nt)):
            mine_after = jnp.where(tm == t, after, mine_after)
            after = early[t, j, 1:2] * after + (late[t, j, 1:2] + early[t, j, 2:3] * entries[t])
        bounds.append((mine, mine_after))

    for j in range(halves):
        at = (last, j)
        mine, mine_after = bounds[j]
        for n in range(last):
            y_copies[n, j].wait_recv()
        state = zeros
        for i in range(steps):
            inflow = um[j, i]
            for n in range(last):
                inflow = inflow + yrecv[n, j, pl.ds(i, SEGS, stride=steps), :]
            state = dm[last, j, i] * state + inflow
            fm[last, j, i] = state
        f_before = shift_rows(chain_rows(p_levels[at], state, 1), 1, 0.0)
        seg_entry = p_before[at] * mine + f_before
        back = zeros
        for i in reversed(range(steps)):
            filtered = fm[last, j, i] + pm[last, j, i] * seg_entry
            filt_v[j, pl.ds(i, SEGS, stride=steps), :] = filtered
            back = gm[last, j, i] * back + cm[last, j, i] * filtered
            am[j, i] = back
        a_after = shift_rows(chain_rows(q_levels[at], back, -1), -1, 0.0)
        seg_after = q_after[at] * mine_after + a_after
        for i in range(steps):
            smooth_v[j, pl.ds(i, SEGS, stride=steps), :] = am[j, i] + qm[j, i] * seg_after
        filt_out[:, j * LANES:(j + 1) * LANES] = filt_v[j]
        smooth_out[:, j * LANES:(j + 1) * LANES] = smooth_v[j]

    for copy in list(core_copies.values()) + list(y_copies.values()):
        copy.wait_send()
    for copy in part_copies + early_copies + late_copies:
        copy.wait_send()


def per_device(nt, ns, observations, obs_list, gain_rows, decay, smooth_gain, model_rate, first_state):
    ny = ns // 2
    hours, depth = observations.shape
    modes = gain_rows.shape[1]
    width = modes // ns
    halves = width // LANES
    steps = hours // SEGS
    f32 = jnp.float32
    dma = pltpu.SemaphoreType.DMA
    any_space = pl.BlockSpec(memory_space=pl.ANY)
    tiles = pltpu.VMEM((halves, steps, SEGS, LANES), f32)
    plane = pltpu.VMEM((halves, hours, LANES), f32)
    planes = pltpu.VMEM((ny, halves, hours, LANES), f32)
    group_tiles = pltpu.VMEM((ny, halves, steps, SEGS, LANES), f32)
    params = pltpu.VMEM((modes // LANES, LANES), f32)
    out = pltpu.VMEM((hours, width), f32)
    vmem_space = pl.BlockSpec(memory_space=pltpu.VMEM)
    return pl.pallas_call(
        functools.partial(kernel, nt, ny),
        out_shape=(out, out),
        in_specs=[any_space] * 7,
        out_specs=(vmem_space, vmem_space),
        scratch_shapes=[
            pltpu.VMEM((hours, depth), jnp.bfloat16),
            pltpu.VMEM(obs_list.shape[::-1], jnp.int32),
            pltpu.VMEM((ny * halves, depth, 2 * LANES), jnp.bfloat16),
            planes, planes, params, params,
            planes, planes, planes, planes,
            tiles, group_tiles, tiles, group_tiles, group_tiles, group_tiles, group_tiles, tiles,
            pltpu.VMEM((nt, halves, 4, LANES), f32),
            pltpu.VMEM((nt, halves, 2, LANES), f32),
            pltpu.VMEM((ny, halves, 2, LANES), f32),
            pltpu.VMEM((ny, halves, 2, LANES), f32),
            plane, plane,
            dma((CHUNKS,)), dma((CHUNKS, 2)), dma((ny * halves, 2)), dma, dma((ny, halves)), dma((ny, halves)), dma((2,)),
            dma((ny, halves)), dma((ny, halves)), dma((ny, halves)), dma((ny, halves)),
            dma((ny,)), dma((ny,)), dma((nt,)), dma((nt,)), dma((nt,)), dma((nt,)),
        ],
        compiler_params=pltpu.CompilerParams(
            collective_id=0, has_side_effects=True, vmem_limit_bytes=56 * 1024 * 1024
        ),
        cost_estimate=pl.CostEstimate(
            flops=2 * hours * depth * modes, bytes_accessed=2 * depth * (hours + modes), transcendentals=0
        ),
    )(
        observations, obs_list.T, gain_rows, decay, smooth_gain,
        model_rate.reshape(modes // LANES, LANES), first_state.reshape(modes // LANES, LANES),
    )


def solution(mesh):
    nt, ns = mesh.shape["tm"], mesh.shape["sensor"]
    in_specs = (
        P("tm", "sensor"),
        P("tm", "sensor"),
        P("sensor", None),
        P("tm", None),
        P("tm", None),
        P(),
        P(),
    )
    out_specs = (P("tm", "sensor"), P("tm", "sensor"))
    return jax.shard_map(
        functools.partial(per_device, nt, ns),
        mesh=mesh, in_specs=in_specs, out_specs=out_specs, check_vma=False,
    )
```

time: 24.5 us -> 25.1 us (1.024)
  Pallas kernels: 22.3 us -> 22.9 us
    pallas_call x1, Pallas kernels: 22.3 us -> 22.9 us  [per_device(): pl.pallas_call(functools.partial(kernel, nt, ny), out_shape=(out, out), i...]
where the time goes in v3:
time: 25.1 us; the launch traced here: 25 us
  Pallas kernels  22.9 us (91%)
  local copies, waits for them, and re-layouts  1.41 us (6%)
  between operations  0.64 us (3%)
    pallas_call x1, Pallas kernels, per_device(): pl.pallas_call(functools.partial(kernel, nt, ny), out_shape=(out, out), i...  22.9 us
    unnamed x2, local copies, waits for them, and re-layouts  1.41 us

profile of v3, /device:TPU:0, one launch (start us, length us, event | category | flops | bytes accessed | tf_op | source)
XLA Modules:
  0.0 25.0 jit_solution(18366663512396583933)
XLA Ops:
  0.6 22.9 %shard_map.86 = (f32[256,256]{1,0:T(8,128)S(1)}, f32[256,256]{1,0:T(8,128)S(1)}) custom-call(bf16[256,4096]{1,0:T(8,128)(2,1)} %obs.1, s32[16,256]{1,0:T(8,128)} %bitcast.3, bf16[4096,1024]{1,0:T(8,128)(2,1)} %gain.1, f32[256,1024]{1,0:T(8,128)} %decay.1, f32[256,1024]{1,0:T(8,128)} %sgain.1, f32[8,128]{1,0:T(8,128)} %bitcast.4, f32[8,128]{1,0:T(8,128)} %bitcast.5), custom_call_target="tpu_custom_call" | custom-call | flops 2147483648 | bytes 10485760 | tf_op jit(solution)/shard_map/pallas_call | solution.py:363
  23.6 0.7 %copy.11 = f32[256,256]{1,0:T(8,128)} copy(f32[256,256]{1,0:T(8,128)S(1)} %get-tuple-element.2) | data formatting | bytes 524288
  24.3 0.7 %copy.12 = f32[256,256]{1,0:T(8,128)} copy(f32[256,256]{1,0:T(8,128)S(1)} %get-tuple-element.3) | data formatting | bytes 524288

commit v4 on v3

--- a/solution.py
+++ b/solution.py
@@ -39,7 +39,7 @@
     filt_out, smooth_out,
     obs_v, list_v, gain_v, dec_v, sg_v, rate_v, first_v,
     csend, crecv, acc, yrecv,
-    um, fm, am, dm, gm, cm, pm, qm,
+    um, fm, am, dm, gm, cm, pm, qm, bm,
     early, late, part_send, part_recv, filt_v, smooth_v,
     obs_sem, gain0_sem, gain_sem, list_sem, dec_sem, sg_sem, par_sem,
     cs_sem, cr_sem, ys_sem, yr_sem, ps_sem, pr_sem, es_sem, er_sem, ls_sem, lr_sem,
@@ -113,24 +113,28 @@
     flat = jnp.broadcast_to(jnp.sum(bit, axis=0, keepdims=True), (LANES, hours))
     bits = jnp.transpose(flat)
 
-    def gate(b, carry):
-        part = pl.ds(pl.multiple_of(b * LANES, LANES), LANES)
-        listed = (bits & lax.shift_left(jnp.int32(1), b)) != 0
-        value = obs_v[:, part].astype(jnp.float32)
-        obs_v[:, part] = jnp.where(listed, value, 0.0).astype(jnp.bfloat16)
-        return carry
+    low_bits = (bits & 0xFFFF).astype(jnp.int16)
+    high_bits = lax.shift_right_logical(bits, 16).astype(jnp.int16)
+
+    def gated(b):
+        part = obs_v[:, b * LANES:(b + 1) * LANES]
+        word, place = (low_bits, b) if b < 16 else (high_bits, b - 16)
+        flag = jnp.int16((1 << place) if place < 15 else -32768)
+        return jnp.where((word & flag) != 0, part, jnp.bfloat16(0))
 
     total = None
     for n in range(CHUNKS):
         obs_copies[n].wait()
-        lax.fori_loop(n * (blocks // CHUNKS), (n + 1) * (blocks // CHUNKS), gate, 0)
         for copy in gain0_copies[n]:
             copy.wait()
         if n == CHUNKS // 2 - 1:
             for copy in gain_copies[pairs[0]]:
                 copy.start()
         part = pl.ds(n * chunk, chunk)
-        term = jnp.dot(obs_v[:, part], gain_v[0, part], preferred_element_type=jnp.float32)
+        per = blocks // CHUNKS
+        weighted = jnp.concatenate([gated(b) for b in range(n * per, (n + 1) * per)], axis=1)
+        obs_v[:, part] = weighted
+        term = jnp.dot(weighted, gain_v[0, part], preferred_element_type=jnp.float32)
         total = term if total is None else total + term
     for copy in steady_copies:
         copy.start()
@@ -151,11 +155,12 @@
         acc[n, j] = total[:, LANES:]
 
     def product(n, j):
-        for copy in gain_copies[n, j]:
-            copy.wait()
-        hand_over(
-            n, j, jnp.dot(obs_v[...], gain_v[n * halves + j], preferred_element_type=jnp.float32)
-        )
+        return jnp.dot(obs_v[...], gain_v[n * halves + j], preferred_element_type=jnp.float32)
+
+    def wait_gain(*pairs):
+        for pair in pairs:
+            for copy in gain_copies[pair]:
+                copy.wait()
 
     def join(n, j):
         core_copies[n, j].wait_recv()
@@ -176,12 +181,12 @@
     hand_over(0, 0, total)
     if away:
         send_y(0, 0)
-    for n, j in away[1:]:
-        product(n, j)
-
+
+    wait_gain(*away[1:])
     for copy in steady_copies:
         copy.wait()
     row_ids = lax.broadcasted_iota(jnp.int32, (SEGS, LANES), 0)
+    products = {at: product(*at) for at in away[1:]}
     last_row = (row_ids == SEGS - 1) & (tm == nt - 1)
     ones = jnp.ones((SEGS, LANES), jnp.float32)
     zeros = jnp.zeros((SEGS, LANES), jnp.float32)
@@ -211,7 +216,8 @@
             cm[n, j, i] = c
             if n == last:
                 qm[j, i] = back[at]
-    p_levels, q_levels, p_before, q_after = {}, {}, {}, {}
+                bm[j, i] = linear[at]
+    p_levels, q_levels, p_before, q_after, b_after = {}, {}, {}, {}, {}
     for at in away + home:
         p_levels[at], p_all = factor_levels(prod[at], 1)
         q_levels[at], q_all = factor_levels(back[at], -1)
@@ -219,12 +225,22 @@
         q_after[at] = shift_rows(q_all, -1, 1.0)
         if at[0] == last:
             b_all = chain_rows(q_levels[at], linear[at] * p_before[at], -1)
+            b_after[at] = shift_rows(b_all, -1, 0.0)
             early[tm, at[1], 0:1] = p_all[SEGS - 1:SEGS]
             early[tm, at[1], 1:2] = q_all[0:1]
             early[tm, at[1], 2:3] = b_all[0:1]
             early[tm, at[1], 3:4] = jnp.zeros((1, LANES), jnp.float32)
     for at in away[1:]:
+        hand_over(*at, products[at])
+    ahead = [at for at in home[:1] if at != (0, 0)]
+    wait_gain(*ahead)
+    for at in ahead:
+        hand_over(*at, product(*at))
+    for at in away[1:]:
         send_y(*at)
+    behind = home[1:]
+    wait_gain(*behind)
+    products = {at: product(*at) for at in behind}
 
     def summaries(group):
         state = {at: zeros for at in group}
@@ -251,6 +267,8 @@
 
     part_copies = []
     away_result = summaries(away)
+    for at in behind:
+        hand_over(*at, products[at])
     for n in range(last):
         for j in range(halves):
             part_send[n, j, 0:1], part_send[n, j, 1:2] = away_result[n, j]
@@ -269,9 +287,6 @@
         copy.start()
         early_copies.append(copy)
 
-    for at in home:
-        if at != (0, 0):
-            product(*at)
     for at in home:
         join(*at)
     home_result = summaries(home)
@@ -292,11 +307,30 @@
         )
         copy.start()
         late_copies.append(copy)
+    f_before, a_after = {}, {}
+    for at in home:
+        j = at[1]
+        for n in range(last):
+            y_copies[n, j].wait_recv()
+        state = zeros
+        for i in range(steps):
+            inflow = um[j, i]
+            for n in range(last):
+                inflow = inflow + yrecv[n, j, pl.ds(i, SEGS, stride=steps), :]
+            state = dm[last, j, i] * state + inflow
+            fm[last, j, i] = state
+        back = zeros
+        for i in reversed(range(steps)):
+            back = gm[last, j, i] * back + cm[last, j, i] * fm[last, j, i]
+            am[j, i] = back
+        f_before[at] = shift_rows(chain_rows(p_levels[at], state, 1), 1, 0.0)
+        a_all = chain_rows(q_levels[at], back + linear[at] * f_before[at], -1)
+        a_after[at] = shift_rows(a_all, -1, 0.0)
+
     for copy in early_copies + late_copies:
         copy.wait_recv()
-
-    bounds = []
-    for j in range(halves):
+    for at in home:
+        j = at[1]
         entry = first_v[pl.ds(sensor * halves + j, 1), :]
         entries, mine = [], entry
         for t in range(nt):
@@ -308,32 +342,12 @@
         for t in reversed(range(nt)):
             mine_after = jnp.where(tm == t, after, mine_after)
             after = early[t, j, 1:2] * after + (late[t, j, 1:2] + early[t, j, 2:3] * entries[t])
-        bounds.append((mine, mine_after))
-
-    for j in range(halves):
-        at = (last, j)
-        mine, mine_after = bounds[j]
-        for n in range(last):
-            y_copies[n, j].wait_recv()
-        state = zeros
+        seg_entry = p_before[at] * mine + f_before[at]
+        seg_after = q_after[at] * mine_after + (a_after[at] + b_after[at] * mine)
         for i in range(steps):
-            inflow = um[j, i]
-            for n in range(last):
-                inflow = inflow + yrecv[n, j, pl.ds(i, SEGS, stride=steps), :]
-            state = dm[last, j, i] * state + inflow
-            fm[last, j, i] = state
-        f_before = shift_rows(chain_rows(p_levels[at], state, 1), 1, 0.0)
-        seg_entry = p_before[at] * mine + f_before
-        back = zeros
-        for i in reversed(range(steps)):
-            filtered = fm[last, j, i] + pm[last, j, i] * seg_entry
-            filt_v[j, pl.ds(i, SEGS, stride=steps), :] = filtered
-            back = gm[last, j, i] * back + cm[last, j, i] * filtered
-            am[j, i] = back
-        a_after = shift_rows(chain_rows(q_levels[at], back, -1), -1, 0.0)
-        seg_after = q_after[at] * mine_after + a_after
-        for i in range(steps):
-            smooth_v[j, pl.ds(i, SEGS, stride=steps), :] = am[j, i] + qm[j, i] * seg_after
+            rows = pl.ds(i, SEGS, stride=steps)
+            filt_v[j, rows, :] = fm[last, j, i] + pm[last, j, i] * seg_entry
+            smooth_v[j, rows, :] = am[j, i] + bm[j, i] * seg_entry + qm[j, i] * seg_after
         filt_out[:, j * LANES:(j + 1) * LANES] = filt_v[j]
         smooth_out[:, j * LANES:(j + 1) * LANES] = smooth_v[j]
 
@@ -371,7 +385,7 @@
             pltpu.VMEM((ny * halves, depth, 2 * LANES), jnp.bfloat16),
             planes, planes, params, params,
             planes, planes, planes, planes,
-            tiles, group_tiles, tiles, group_tiles, group_tiles, group_tiles, group_tiles, tiles,
+            tiles, group_tiles, tiles, group_tiles, group_tiles, group_tiles, group_tiles, tiles, tiles,
             pltpu.VMEM((nt, halves, 4, LANES), f32),
             pltpu.VMEM((nt, halves, 2, LANES), f32),
             pltpu.VMEM((ny, halves, 2, LANES), f32),

time: 25.1 us -> 25 us (level)
  no operation moved by 1% of the time
where the time goes in v4:
time: 25 us; the launch traced here: 24.9 us
  Pallas kernels  22.8 us (91%)
  local copies, waits for them, and re-layouts  1.41 us (6%)
  between operations  0.64 us (3%)
    pallas_call x1, Pallas kernels, per_device(): pl.pallas_call(functools.partial(kernel, nt, ny), out_shape=(out, out), i...  22.8 us
    unnamed x2, local copies, waits for them, and re-layouts  1.41 us

profile of v4, /device:TPU:0, one launch (start us, length us, event | category | flops | bytes accessed | tf_op | source)
XLA Modules:
  0.0 24.9 jit_solution(5588170906863978872)
XLA Ops:
  0.6 22.8 %shard_map.86 = (f32[256,256]{1,0:T(8,128)S(1)}, f32[256,256]{1,0:T(8,128)S(1)}) custom-call(bf16[256,4096]{1,0:T(8,128)(2,1)} %obs.1, s32[16,256]{1,0:T(8,128)} %bitcast.3, bf16[4096,1024]{1,0:T(8,128)(2,1)} %gain.1, f32[256,1024]{1,0:T(8,128)} %decay.1, f32[256,1024]{1,0:T(8,128)} %sgain.1, f32[8,128]{1,0:T(8,128)} %bitcast.4, f32[8,128]{1,0:T(8,128)} %bitcast.5), custom_call_target="tpu_custom_call" | custom-call | flops 2147483648 | bytes 10485760 | tf_op jit(solution)/shard_map/pallas_call | solution.py:377
  23.5 0.7 %copy.11 = f32[256,256]{1,0:T(8,128)} copy(f32[256,256]{1,0:T(8,128)S(1)} %get-tuple-element.2) | data formatting | bytes 524288
  24.2 0.7 %copy.12 = f32[256,256]{1,0:T(8,128)} copy(f32[256,256]{1,0:T(8,128)S(1)} %get-tuple-element.3) | data formatting | bytes 524288

commit v5 on v4

--- a/solution.py
+++ b/solution.py
@@ -9,6 +9,7 @@
 LANES = 128
 SEGS = 8
 CHUNKS = 4
+UNROLL = 4
 MESH = pl.DeviceIdType.MESH
 
 
@@ -31,6 +32,16 @@
     for level, count in zip(levels, (1, 2, 4)):
         value = value + level * shift_rows(value, sign * count, 0.0)
     return value
+
+
+def hours_loop(steps, body, carry, reverse=False):
+    def group(n, carry):
+        for u in range(UNROLL):
+            i = n * UNROLL + u
+            carry = body(steps - 1 - i if reverse else i, carry)
+        return carry
+
+    return lax.fori_loop(0, steps // UNROLL, group, carry)
 
 
 def kernel(
@@ -40,7 +51,7 @@
     obs_v, list_v, gain_v, dec_v, sg_v, rate_v, first_v,
     csend, crecv, acc, yrecv,
     um, fm, am, dm, gm, cm, pm, qm, bm,
-    early, late, part_send, part_recv, filt_v, smooth_v,
+    early, late, part_send, part_recv, filt_v, smooth_v, total_v,
     obs_sem, gain0_sem, gain_sem, list_sem, dec_sem, sg_sem, par_sem,
     cs_sem, cr_sem, ys_sem, yr_sem, ps_sem, pr_sem, es_sem, er_sem, ls_sem, lr_sem,
 ):
@@ -113,29 +124,39 @@
     flat = jnp.broadcast_to(jnp.sum(bit, axis=0, keepdims=True), (LANES, hours))
     bits = jnp.transpose(flat)
 
-    low_bits = (bits & 0xFFFF).astype(jnp.int16)
-    high_bits = lax.shift_right_logical(bits, 16).astype(jnp.int16)
-
-    def gated(b):
-        part = obs_v[:, b * LANES:(b + 1) * LANES]
-        word, place = (low_bits, b) if b < 16 else (high_bits, b - 16)
-        flag = jnp.int16((1 << place) if place < 15 else -32768)
-        return jnp.where((word & flag) != 0, part, jnp.bfloat16(0))
-
-    total = None
-    for n in range(CHUNKS):
-        obs_copies[n].wait()
-        for copy in gain0_copies[n]:
+    per = blocks // CHUNKS
+
+    def first_chunk(n, carry):
+        start = pl.multiple_of(n * chunk, chunk)
+        part = pl.ds(start, chunk)
+        pltpu.make_async_copy(obs.at[:, part], obs_v.at[:, part], obs_sem.at[n]).wait()
+        word = lax.shift_right_logical(bits, n * per).astype(jnp.int16)
+        pieces = []
+        for b in range(per):
+            piece = obs_v[:, pl.ds(pl.multiple_of(start + b * LANES, LANES), LANES)]
+            pieces.append(jnp.where((word & jnp.int16(1 << b)) != 0, piece, jnp.bfloat16(0)))
+        weighted = jnp.concatenate(pieces, axis=1)
+        obs_v[:, part] = weighted
+        for copy in gain_pair(0, 0, part, gain0_sem.at[n]):
             copy.wait()
-        if n == CHUNKS // 2 - 1:
+        term = jnp.dot(weighted, gain_v[0, part], preferred_element_type=jnp.float32)
+
+        @pl.when(n == 0)
+        def _():
+            total_v[...] = term
+
+        @pl.when(n > 0)
+        def _():
+            total_v[...] += term
+
+        @pl.when(n == CHUNKS // 2 - 1)
+        def _():
             for copy in gain_copies[pairs[0]]:
                 copy.start()
-        part = pl.ds(n * chunk, chunk)
-        per = blocks // CHUNKS
-        weighted = jnp.concatenate([gated(b) for b in range(n * per, (n + 1) * per)], axis=1)
-        obs_v[:, part] = weighted
-        term = jnp.dot(weighted, gain_v[0, part], preferred_element_type=jnp.float32)
-        total = term if total is None else total + term
+
+        return carry
+
+    lax.fori_loop(0, CHUNKS, first_chunk, 0)
     for copy in steady_copies:
         copy.start()
     for pair in pairs[1:]:
@@ -144,18 +165,28 @@
 
     core_copies, y_copies = {}, {}
 
-    def hand_over(n, j, total):
-        csend[n, j] = total[:, :LANES]
+    def hand_over(n, j):
+        csend[n, j] = total_v[:, :LANES]
         copy = pltpu.make_async_remote_copy(
             csend.at[n, j], crecv.at[n, j], cs_sem.at[n, j], cr_sem.at[n, j],
             device_id=(tm, partner), device_id_type=MESH,
         )
         copy.start()
         core_copies[n, j] = copy
-        acc[n, j] = total[:, LANES:]
+        acc[n, j] = total_v[:, LANES:]
 
     def product(n, j):
-        return jnp.dot(obs_v[...], gain_v[n * halves + j], preferred_element_type=jnp.float32)
+        total_v[...] = jnp.zeros_like(total_v)
+
+        def add(m, carry):
+            part = pl.ds(pl.multiple_of(m * chunk, chunk), chunk)
+            total_v[...] += jnp.dot(
+                obs_v[:, part], gain_v[n * halves + j, part], preferred_element_type=jnp.float32
+            )
+            return carry
+
+        lax.fori_loop(0, CHUNKS, add, 0)
+        hand_over(n, j)
 
     def wait_gain(*pairs):
         for pair in pairs:
@@ -178,15 +209,16 @@
     away = [(n, j) for n in range(last) for j in range(halves)]
     home = [(last, j) for j in range(halves)]
     pl.semaphore_wait(barrier, len(peers))
-    hand_over(0, 0, total)
+    hand_over(0, 0)
     if away:
         send_y(0, 0)
 
     wait_gain(*away[1:])
+    for at in away[1:]:
+        product(*at)
     for copy in steady_copies:
         copy.wait()
     row_ids = lax.broadcasted_iota(jnp.int32, (SEGS, LANES), 0)
-    products = {at: product(*at) for at in away[1:]}
     last_row = (row_ids == SEGS - 1) & (tm == nt - 1)
     ones = jnp.ones((SEGS, LANES), jnp.float32)
     zeros = jnp.zeros((SEGS, LANES), jnp.float32)
@@ -194,29 +226,41 @@
         (n, j): jnp.broadcast_to(rate_v[pl.ds(mine_at(shifts[n]) * halves + j, 1), :], (SEGS, LANES))
         for n, j in away + home
     }
-    prod = {at: ones for at in away + home}
-    for i in range(steps):
-        for at in away + home:
-            d = dec_v[at[0], at[1], pl.ds(i, SEGS, stride=steps), :]
-            prod[at] = d * prod[at]
-            dm[at[0], at[1], i] = d
-            pm[at[0], at[1], i] = prod[at]
-    back = {at: ones for at in away + home}
-    linear = {at: zeros for at in away + home}
-    for i in reversed(range(steps)):
-        for at in away + home:
+    spots = away + home
+
+    def forward_factors(i, prods):
+        out = []
+        for (n, j), prod in zip(spots, prods):
+            d = dec_v[n, j, pl.ds(i, SEGS, stride=steps), :]
+            prod = d * prod
+            dm[n, j, i] = d
+            pm[n, j, i] = prod
+            out.append(prod)
+        return tuple(out)
+
+    prods = hours_loop(steps, forward_factors, (ones,) * len(spots))
+
+    def backward_factors(i, pairs):
+        out = []
+        for at, (line, factor) in zip(spots, pairs):
             n, j = at
             g = sg_v[n, j, pl.ds(i, SEGS, stride=steps), :]
-            if i == steps - 1:
-                g = jnp.where(last_row, 0.0, g)
+            g = jnp.where(last_row & (i == steps - 1), 0.0, g)
             c = 1.0 - g * rates[at]
-            linear[at] = g * linear[at] + c * pm[n, j, i]
-            back[at] = g * back[at]
+            line = g * line + c * pm[n, j, i]
+            factor = g * factor
             gm[n, j, i] = g
             cm[n, j, i] = c
             if n == last:
-                qm[j, i] = back[at]
-                bm[j, i] = linear[at]
+                qm[j, i] = factor
+                bm[j, i] = line
+            out.append((line, factor))
+        return tuple(out)
+
+    factors = hours_loop(steps, backward_factors, ((zeros, ones),) * len(spots), reverse=True)
+    prod = dict(zip(spots, prods))
+    linear = {at: line for at, (line, _) in zip(spots, factors)}
+    back = {at: factor for at, (_, factor) in zip(spots, factors)}
     p_levels, q_levels, p_before, q_after, b_after = {}, {}, {}, {}, {}
     for at in away + home:
         p_levels[at], p_all = factor_levels(prod[at], 1)
@@ -230,33 +274,38 @@
             early[tm, at[1], 1:2] = q_all[0:1]
             early[tm, at[1], 2:3] = b_all[0:1]
             early[tm, at[1], 3:4] = jnp.zeros((1, LANES), jnp.float32)
-    for at in away[1:]:
-        hand_over(*at, products[at])
     ahead = [at for at in home[:1] if at != (0, 0)]
     wait_gain(*ahead)
     for at in ahead:
-        hand_over(*at, product(*at))
+        product(*at)
     for at in away[1:]:
         send_y(*at)
     behind = home[1:]
     wait_gain(*behind)
-    products = {at: product(*at) for at in behind}
+    for at in behind:
+        product(*at)
 
     def summaries(group):
-        state = {at: zeros for at in group}
-        for i in range(steps):
-            for at in group:
-                n, j = at
+        def forward(i, states):
+            out = []
+            for (n, j), state in zip(group, states):
                 inflow = acc[n, j, pl.ds(i, SEGS, stride=steps), :]
                 if n == last:
                     um[j, i] = inflow
-                state[at] = dm[n, j, i] * state[at] + inflow
-                fm[n, j, i] = state[at]
-        back = {at: zeros for at in group}
-        for i in reversed(range(steps)):
-            for at in group:
-                n, j = at
-                back[at] = gm[n, j, i] * back[at] + cm[n, j, i] * fm[n, j, i]
+                state = dm[n, j, i] * state + inflow
+                fm[n, j, i] = state
+                out.append(state)
+            return tuple(out)
+
+        states = hours_loop(steps, forward, (zeros,) * len(group))
+
+        def backward(i, backs):
+            return tuple(
+                gm[n, j, i] * back + cm[n, j, i] * fm[n, j, i] for (n, j), back in zip(group, backs)
+            )
+
+        backs = hours_loop(steps, backward, (zeros,) * len(group), reverse=True)
+        state, back = dict(zip(group, states)), dict(zip(group, backs))
         result = {}
         for at in group:
             f_all = chain_rows(p_levels[at], state[at], 1)
@@ -267,8 +316,6 @@
 
     part_copies = []
     away_result = summaries(away)
-    for at in behind:
-        hand_over(*at, products[at])
     for n in range(last):
         for j in range(halves):
             part_send[n, j, 0:1], part_send[n, j, 1:2] = away_result[n, j]
@@ -312,17 +359,22 @@
         j = at[1]
         for n in range(last):
             y_copies[n, j].wait_recv()
-        state = zeros
-        for i in range(steps):
+
+        def forward(i, state, j=j):
             inflow = um[j, i]
             for n in range(last):
                 inflow = inflow + yrecv[n, j, pl.ds(i, SEGS, stride=steps), :]
             state = dm[last, j, i] * state + inflow
             fm[last, j, i] = state
-        back = zeros
-        for i in reversed(range(steps)):
+            return state
+
+        def backward(i, back, j=j):
             back = gm[last, j, i] * back + cm[last, j, i] * fm[last, j, i]
             am[j, i] = back
+            return back
+
+        state = hours_loop(steps, forward, zeros)
+        back = hours_loop(steps, backward, zeros, reverse=True)
         f_before[at] = shift_rows(chain_rows(p_levels[at], state, 1), 1, 0.0)
         a_all = chain_rows(q_levels[at], back + linear[at] * f_before[at], -1)
         a_after[at] = shift_rows(a_all, -1, 0.0)
@@ -344,10 +396,14 @@
             after = early[t, j, 1:2] * after + (late[t, j, 1:2] + early[t, j, 2:3] * entries[t])
         seg_entry = p_before[at] * mine + f_before[at]
         seg_after = q_after[at] * mine_after + (a_after[at] + b_after[at] * mine)
-        for i in range(steps):
+
+        def finish(i, carry, j=j, seg_entry=seg_entry, seg_after=seg_after):
             rows = pl.ds(i, SEGS, stride=steps)
             filt_v[j, rows, :] = fm[last, j, i] + pm[last, j, i] * seg_entry
             smooth_v[j, rows, :] = am[j, i] + bm[j, i] * seg_entry + qm[j, i] * seg_after
+            return carry
+
+        hours_loop(steps, finish, 0)
         filt_out[:, j * LANES:(j + 1) * LANES] = filt_v[j]
         smooth_out[:, j * LANES:(j + 1) * LANES] = smooth_v[j]
 
@@ -390,7 +446,7 @@
             pltpu.VMEM((nt, halves, 2, LANES), f32),
             pltpu.VMEM((ny, halves, 2, LANES), f32),
             pltpu.VMEM((ny, halves, 2, LANES), f32),
-            plane, plane,
+            plane, plane, pltpu.VMEM((hours, 2 * LANES), f32),
             dma((CHUNKS,)), dma((CHUNKS, 2)), dma((ny * halves, 2)), dma, dma((ny, halves)), dma((ny, halves)), dma((2,)),
             dma((ny, halves)), dma((ny, halves)), dma((ny, halves)), dma((ny, halves)),
             dma((ny,)), dma((ny,)), dma((nt,)), dma((nt,)), dma((nt,)), dma((nt,)),

time: 25 us -> 25.6 us (1.024)
  Pallas kernels: 22.8 us -> 23.4 us
    pallas_call x1, Pallas kernels: 22.8 us -> 23.4 us  [per_device(): pl.pallas_call(functools.partial(kernel, nt, ny), out_shape=(out, out), i...]
where the time goes in v5:
time: 25.6 us; the launch traced here: 25.5 us
  Pallas kernels  23.4 us (91%)
  local copies, waits for them, and re-layouts  1.41 us (6%)
  between operations  0.64 us (2%)
    pallas_call x1, Pallas kernels, per_device(): pl.pallas_call(functools.partial(kernel, nt, ny), out_shape=(out, out), i...  23.4 us
    unnamed x2, local copies, waits for them, and re-layouts  1.41 us

profile of v5, /device:TPU:0, one launch (start us, length us, event | category | flops | bytes accessed | tf_op | source)
XLA Modules:
  0.0 25.5 jit_solution(10618367994581617982)
XLA Ops:
  0.6 23.4 %shard_map.86 = (f32[256,256]{1,0:T(8,128)S(1)}, f32[256,256]{1,0:T(8,128)S(1)}) custom-call(bf16[256,4096]{1,0:T(8,128)(2,1)} %obs.1, s32[16,256]{1,0:T(8,128)} %bitcast.3, bf16[4096,1024]{1,0:T(8,128)(2,1)} %gain.1, f32[256,1024]{1,0:T(8,128)} %decay.1, f32[256,1024]{1,0:T(8,128)} %sgain.1, f32[8,128]{1,0:T(8,128)} %bitcast.4, f32[8,128]{1,0:T(8,128)} %bitcast.5), custom_call_target="tpu_custom_call" | custom-call | flops 2147483648 | bytes 10485760 | tf_op jit(solution)/shard_map/pallas_call | solution.py:433
  24.1 0.7 %copy.11 = f32[256,256]{1,0:T(8,128)} copy(f32[256,256]{1,0:T(8,128)S(1)} %get-tuple-element.2) | data formatting | bytes 524288
  24.8 0.7 %copy.12 = f32[256,256]{1,0:T(8,128)} copy(f32[256,256]{1,0:T(8,128)S(1)} %get-tuple-element.3) | data formatting | bytes 524288

commit v6 on v4

--- a/solution.py
+++ b/solution.py
@@ -38,7 +38,7 @@
     obs, olist, gain, decay, sgain, rate, first,
     filt_out, smooth_out,
     obs_v, list_v, gain_v, dec_v, sg_v, rate_v, first_v,
-    csend, crecv, acc, yrecv,
+    total_v, crecv, acc, yrecv,
     um, fm, am, dm, gm, cm, pm, qm, bm,
     early, late, part_send, part_recv, filt_v, smooth_v,
     obs_sem, gain0_sem, gain_sem, list_sem, dec_sem, sg_sem, par_sem,
@@ -64,16 +64,9 @@
     def columns(dest, j):
         return pl.ds(pl.multiple_of(dest * width + j * LANES, LANES), LANES)
 
-    def gain_pair(n, j, rows, sems):
-        own = mine_at(shifts[n])
-        other = own + 1 - 2 * core
-        slot = gain_v.at[n * halves + j]
-        return [
-            pltpu.make_async_copy(
-                gain.at[rows, columns(dest, j)], slot.at[rows, pl.ds(side * LANES, LANES)], sems.at[side]
-            )
-            for side, dest in enumerate((other, own))
-        ]
+    def gain_copy(n, rows, sem):
+        here = pl.ds(pl.multiple_of(lax.rem(y + shifts[n], ny) * 2 * width, LANES), 2 * width)
+        return pltpu.make_async_copy(gain.at[rows, here], gain_v.at[n, rows], sem)
 
     list_copy = pltpu.make_async_copy(olist, list_v, list_sem)
     list_copy.start()
@@ -81,15 +74,11 @@
     for n in range(CHUNKS):
         part = pl.ds(n * chunk, chunk)
         obs_copies.append(pltpu.make_async_copy(obs.at[:, part], obs_v.at[:, part], obs_sem.at[n]))
-        gain0_copies.append(gain_pair(0, 0, part, gain0_sem.at[n]))
-        for copy in [obs_copies[-1]] + gain0_copies[-1]:
-            copy.start()
+        gain0_copies.append(gain_copy(0, part, gain0_sem.at[n]))
+        obs_copies[-1].start()
+        gain0_copies[-1].start()
     everything = pl.ds(0, depth)
-    gain_copies = {
-        (n, j): gain_pair(n, j, everything, gain_sem.at[n * halves + j])
-        for n in range(ny) for j in range(halves) if n + j > 0
-    }
-    pairs = list(gain_copies)
+    gain_copies = {n: gain_copy(n, everything, gain_sem.at[n]) for n in range(1, ny)}
     steady_copies = []
     for n in range(ny):
         for j in range(halves):
@@ -125,46 +114,38 @@
     total = None
     for n in range(CHUNKS):
         obs_copies[n].wait()
-        for copy in gain0_copies[n]:
-            copy.wait()
-        if n == CHUNKS // 2 - 1:
-            for copy in gain_copies[pairs[0]]:
-                copy.start()
+        gain0_copies[n].wait()
         part = pl.ds(n * chunk, chunk)
         per = blocks // CHUNKS
         weighted = jnp.concatenate([gated(b) for b in range(n * per, (n + 1) * per)], axis=1)
         obs_v[:, part] = weighted
         term = jnp.dot(weighted, gain_v[0, part], preferred_element_type=jnp.float32)
         total = term if total is None else total + term
-    for copy in steady_copies:
-        copy.start()
-    for pair in pairs[1:]:
-        for copy in gain_copies[pair]:
+        if n == CHUNKS // 2 - 1:
+            for copy in steady_copies + list(gain_copies.values()):
+                copy.start()
+
+    core_copies, y_copies = {}, {}
+
+    def hand_over(n, total):
+        for side in range(2):
+            for j in range(halves):
+                at = (side * halves + j) * LANES
+                total_v[n, side, j] = total[:, at:at + LANES]
+        for j in range(halves):
+            copy = pltpu.make_async_remote_copy(
+                total_v.at[n, 1 - core, j], crecv.at[n, j], cs_sem.at[n, j], cr_sem.at[n, j],
+                device_id=(tm, partner), device_id_type=MESH,
+            )
             copy.start()
-
-    core_copies, y_copies = {}, {}
-
-    def hand_over(n, j, total):
-        csend[n, j] = total[:, :LANES]
-        copy = pltpu.make_async_remote_copy(
-            csend.at[n, j], crecv.at[n, j], cs_sem.at[n, j], cr_sem.at[n, j],
-            device_id=(tm, partner), device_id_type=MESH,
-        )
-        copy.start()
-        core_copies[n, j] = copy
-        acc[n, j] = total[:, LANES:]
-
-    def product(n, j):
-        return jnp.dot(obs_v[...], gain_v[n * halves + j], preferred_element_type=jnp.float32)
-
-    def wait_gain(*pairs):
-        for pair in pairs:
-            for copy in gain_copies[pair]:
-                copy.wait()
+            core_copies[n, j] = copy
+
+    def product(n):
+        return jnp.dot(obs_v[...], gain_v[n], preferred_element_type=jnp.float32)
 
     def join(n, j):
         core_copies[n, j].wait_recv()
-        acc[n, j] = acc[n, j] + crecv[n, j]
+        acc[n, j] = total_v[n, core, j] + crecv[n, j]
 
     def send_y(n, j):
         join(n, j)
@@ -178,15 +159,22 @@
     away = [(n, j) for n in range(last) for j in range(halves)]
     home = [(last, j) for j in range(halves)]
     pl.semaphore_wait(barrier, len(peers))
-    hand_over(0, 0, total)
-    if away:
-        send_y(0, 0)
-
-    wait_gain(*away[1:])
+    hand_over(0, total)
+    for at in away[:halves]:
+        send_y(*at)
+    for n in range(1, last):
+        gain_copies[n].wait()
+        hand_over(n, product(n))
+        for j in range(halves):
+            send_y(n, j)
+    if last > 0:
+        gain_copies[last].wait()
+
     for copy in steady_copies:
         copy.wait()
     row_ids = lax.broadcasted_iota(jnp.int32, (SEGS, LANES), 0)
-    products = {at: product(*at) for at in away[1:]}
+    if last > 0:
+        total = product(last)
     last_row = (row_ids == SEGS - 1) & (tm == nt - 1)
     ones = jnp.ones((SEGS, LANES), jnp.float32)
     zeros = jnp.zeros((SEGS, LANES), jnp.float32)
@@ -230,17 +218,8 @@
             early[tm, at[1], 1:2] = q_all[0:1]
             early[tm, at[1], 2:3] = b_all[0:1]
             early[tm, at[1], 3:4] = jnp.zeros((1, LANES), jnp.float32)
-    for at in away[1:]:
-        hand_over(*at, products[at])
-    ahead = [at for at in home[:1] if at != (0, 0)]
-    wait_gain(*ahead)
-    for at in ahead:
-        hand_over(*at, product(*at))
-    for at in away[1:]:
-        send_y(*at)
-    behind = home[1:]
-    wait_gain(*behind)
-    products = {at: product(*at) for at in behind}
+    if last > 0:
+        hand_over(last, total)
 
     def summaries(group):
         state = {at: zeros for at in group}
@@ -267,8 +246,6 @@
 
     part_copies = []
     away_result = summaries(away)
-    for at in behind:
-        hand_over(*at, products[at])
     for n in range(last):
         for j in range(halves):
             part_send[n, j, 0:1], part_send[n, j, 1:2] = away_result[n, j]
@@ -382,16 +359,16 @@
         scratch_shapes=[
             pltpu.VMEM((hours, depth), jnp.bfloat16),
             pltpu.VMEM(obs_list.shape[::-1], jnp.int32),
-            pltpu.VMEM((ny * halves, depth, 2 * LANES), jnp.bfloat16),
+            pltpu.VMEM((ny, depth, 2 * width), jnp.bfloat16),
             planes, planes, params, params,
-            planes, planes, planes, planes,
+            pltpu.VMEM((ny, 2, halves, hours, LANES), f32), planes, planes, planes,
             tiles, group_tiles, tiles, group_tiles, group_tiles, group_tiles, group_tiles, tiles, tiles,
             pltpu.VMEM((nt, halves, 4, LANES), f32),
             pltpu.VMEM((nt, halves, 2, LANES), f32),
             pltpu.VMEM((ny, halves, 2, LANES), f32),
             pltpu.VMEM((ny, halves, 2, LANES), f32),
             plane, plane,
-            dma((CHUNKS,)), dma((CHUNKS, 2)), dma((ny * halves, 2)), dma, dma((ny, halves)), dma((ny, halves)), dma((2,)),
+            dma((CHUNKS,)), dma((CHUNKS,)), dma((ny,)), dma, dma((ny, halves)), dma((ny, halves)), dma((2,)),
             dma((ny, halves)), dma((ny, halves)), dma((ny, halves)), dma((ny, halves)),
             dma((ny,)), dma((ny,)), dma((nt,)), dma((nt,)), dma((nt,)), dma((nt,)),
         ],

time: 25 us -> 24.2 us (0.968)
  Pallas kernels: 22.8 us -> 22 us
    pallas_call x1, Pallas kernels: 22.8 us -> 22 us  [per_device(): pl.pallas_call(functools.partial(kernel, nt, ny), out_shape=(out, out), i...]
where the time goes in v6:
time: 24.2 us; the launch traced here: 24 us
  Pallas kernels  22 us (91%)
  local copies, waits for them, and re-layouts  1.41 us (6%)
  between operations  0.64 us (3%)
    pallas_call x1, Pallas kernels, per_device(): pl.pallas_call(functools.partial(kernel, nt, ny), out_shape=(out, out), i...  22 us
    unnamed x2, local copies, waits for them, and re-layouts  1.41 us

profile of v6, /device:TPU:0, one launch (start us, length us, event | category | flops | bytes accessed | tf_op | source)
XLA Modules:
  0.0 24.0 jit_solution(12445557994335897105)
XLA Ops:
  0.6 22.0 %shard_map.86 = (f32[256,256]{1,0:T(8,128)S(1)}, f32[256,256]{1,0:T(8,128)S(1)}) custom-call(bf16[256,4096]{1,0:T(8,128)(2,1)} %obs.1, s32[16,256]{1,0:T(8,128)} %bitcast.3, bf16[4096,1024]{1,0:T(8,128)(2,1)} %gain.1, f32[256,1024]{1,0:T(8,128)} %decay.1, f32[256,1024]{1,0:T(8,128)} %sgain.1, f32[8,128]{1,0:T(8,128)} %bitcast.4, f32[8,128]{1,0:T(8,128)} %bitcast.5), custom_call_target="tpu_custom_call" | custom-call | flops 2147483648 | bytes 10485760 | tf_op jit(solution)/shard_map/pallas_call | solution.py:354
  22.6 0.7 %copy.11 = f32[256,256]{1,0:T(8,128)} copy(f32[256,256]{1,0:T(8,128)S(1)} %get-tuple-element.2) | data formatting | bytes 524288
  23.3 0.7 %copy.12 = f32[256,256]{1,0:T(8,128)} copy(f32[256,256]{1,0:T(8,128)S(1)} %get-tuple-element.3) | data formatting | bytes 524288

commit v7 on v6

--- a/solution.py
+++ b/solution.py
@@ -9,6 +9,7 @@
 LANES = 128
 SEGS = 8
 CHUNKS = 4
+PIECES = 4
 MESH = pl.DeviceIdType.MESH
 
 
@@ -149,12 +150,16 @@
 
     def send_y(n, j):
         join(n, j)
-        copy = pltpu.make_async_remote_copy(
-            acc.at[n, j], yrecv.at[n, j], ys_sem.at[n, j], yr_sem.at[n, j],
-            device_id=(tm, mine_at(shifts[n])), device_id_type=MESH,
-        )
-        copy.start()
-        y_copies[n, j] = copy
+        y_copies[n, j] = []
+        for piece in range(PIECES):
+            rows = pl.ds(piece * (hours // PIECES), hours // PIECES)
+            copy = pltpu.make_async_remote_copy(
+                acc.at[n, j, rows], yrecv.at[n, j, rows],
+                ys_sem.at[n, j, piece], yr_sem.at[n, j, piece],
+                device_id=(tm, mine_at(shifts[n])), device_id_type=MESH,
+            )
+            copy.start()
+            y_copies[n, j].append(copy)
 
     away = [(n, j) for n in range(last) for j in range(halves)]
     home = [(last, j) for j in range(halves)]
@@ -284,24 +289,28 @@
         )
         copy.start()
         late_copies.append(copy)
-    f_before, a_after = {}, {}
-    for at in home:
-        j = at[1]
-        for n in range(last):
-            y_copies[n, j].wait_recv()
-        state = zeros
-        for i in range(steps):
+    for pieces in y_copies.values():
+        for copy in pieces:
+            copy.wait_recv()
+    state = {at: zeros for at in home}
+    for i in range(steps):
+        for at in home:
+            j = at[1]
             inflow = um[j, i]
             for n in range(last):
                 inflow = inflow + yrecv[n, j, pl.ds(i, SEGS, stride=steps), :]
-            state = dm[last, j, i] * state + inflow
-            fm[last, j, i] = state
-        back = zeros
-        for i in reversed(range(steps)):
-            back = gm[last, j, i] * back + cm[last, j, i] * fm[last, j, i]
-            am[j, i] = back
-        f_before[at] = shift_rows(chain_rows(p_levels[at], state, 1), 1, 0.0)
-        a_all = chain_rows(q_levels[at], back + linear[at] * f_before[at], -1)
+            state[at] = dm[last, j, i] * state[at] + inflow
+            fm[last, j, i] = state[at]
+    back = {at: zeros for at in home}
+    for i in reversed(range(steps)):
+        for at in home:
+            j = at[1]
+            back[at] = gm[last, j, i] * back[at] + cm[last, j, i] * fm[last, j, i]
+            am[j, i] = back[at]
+    f_before, a_after = {}, {}
+    for at in home:
+        f_before[at] = shift_rows(chain_rows(p_levels[at], state[at], 1), 1, 0.0)
+        a_all = chain_rows(q_levels[at], back[at] + linear[at] * f_before[at], -1)
         a_after[at] = shift_rows(a_all, -1, 0.0)
 
     for copy in early_copies + late_copies:
@@ -328,7 +337,7 @@
         filt_out[:, j * LANES:(j + 1) * LANES] = filt_v[j]
         smooth_out[:, j * LANES:(j + 1) * LANES] = smooth_v[j]
 
-    for copy in list(core_copies.values()) + list(y_copies.values()):
+    for copy in list(core_copies.values()) + sum(y_copies.values(), []):
         copy.wait_send()
     for copy in part_copies + early_copies + late_copies:
         copy.wait_send()
@@ -369,7 +378,7 @@
             pltpu.VMEM((ny, halves, 2, LANES), f32),
             plane, plane,
             dma((CHUNKS,)), dma((CHUNKS,)), dma((ny,)), dma, dma((ny, halves)), dma((ny, halves)), dma((2,)),
-            dma((ny, halves)), dma((ny, halves)), dma((ny, halves)), dma((ny, halves)),
+            dma((ny, halves)), dma((ny, halves)), dma((ny, halves, PIECES)), dma((ny, halves, PIECES)),
             dma((ny,)), dma((ny,)), dma((nt,)), dma((nt,)), dma((nt,)), dma((nt,)),
         ],
         compiler_params=pltpu.CompilerParams(

time: 24.2 us -> 24.4 us (level)
  no operation moved by 1% of the time
where the time goes in v7:
time: 24.4 us; the launch traced here: 24.2 us
  Pallas kernels  22.2 us (91%)
  local copies, waits for them, and re-layouts  1.41 us (6%)
  between operations  0.64 us (3%)
    pallas_call x1, Pallas kernels, per_device(): pl.pallas_call(functools.partial(kernel, nt, ny), out_shape=(out, out), i...  22.2 us
    unnamed x2, local copies, waits for them, and re-layouts  1.41 us

profile of v7, /device:TPU:0, one launch (start us, length us, event | category | flops | bytes accessed | tf_op | source)
XLA Modules:
  0.0 24.2 jit_solution(6541587570888115471)
XLA Ops:
  0.6 22.2 %shard_map.86 = (f32[256,256]{1,0:T(8,128)S(1)}, f32[256,256]{1,0:T(8,128)S(1)}) custom-call(bf16[256,4096]{1,0:T(8,128)(2,1)} %obs.1, s32[16,256]{1,0:T(8,128)} %bitcast.3, bf16[4096,1024]{1,0:T(8,128)(2,1)} %gain.1, f32[256,1024]{1,0:T(8,128)} %decay.1, f32[256,1024]{1,0:T(8,128)} %sgain.1, f32[8,128]{1,0:T(8,128)} %bitcast.4, f32[8,128]{1,0:T(8,128)} %bitcast.5), custom_call_target="tpu_custom_call" | custom-call | flops 2147483648 | bytes 10485760 | tf_op jit(solution)/shard_map/pallas_call | solution.py:363
  22.8 0.7 %copy.11 = f32[256,256]{1,0:T(8,128)} copy(f32[256,256]{1,0:T(8,128)S(1)} %get-tuple-element.2) | data formatting | bytes 524288
  23.5 0.7 %copy.12 = f32[256,256]{1,0:T(8,128)} copy(f32[256,256]{1,0:T(8,128)S(1)} %get-tuple-element.3) | data formatting | bytes 524288

commit v8 on v6

--- a/solution.py
+++ b/solution.py
@@ -39,10 +39,10 @@
     filt_out, smooth_out,
     obs_v, list_v, gain_v, dec_v, sg_v, rate_v, first_v,
     total_v, crecv, acc, yrecv,
-    um, fm, am, dm, gm, cm, pm, qm, bm,
-    early, late, part_send, part_recv, filt_v, smooth_v,
+    fm, am, dm, gm, cm, pm, qm, bm,
+    early, late, filt_v, smooth_v,
     obs_sem, gain0_sem, gain_sem, list_sem, dec_sem, sg_sem, par_sem,
-    cs_sem, cr_sem, ys_sem, yr_sem, ps_sem, pr_sem, es_sem, er_sem, ls_sem, lr_sem,
+    cs_sem, cr_sem, ys_sem, yr_sem, es_sem, er_sem, ls_sem, lr_sem,
 ):
     tm = lax.axis_index("tm")
     sensor = lax.axis_index("sensor")
@@ -80,7 +80,7 @@
     everything = pl.ds(0, depth)
     gain_copies = {n: gain_copy(n, everything, gain_sem.at[n]) for n in range(1, ny)}
     steady_copies = []
-    for n in range(ny):
+    for n in (last,):
         for j in range(halves):
             here = columns(mine_at(shifts[n]), j)
             steady_copies.append(pltpu.make_async_copy(decay.at[:, here], dec_v.at[n, j], dec_sem.at[n, j]))
@@ -180,19 +180,19 @@
     zeros = jnp.zeros((SEGS, LANES), jnp.float32)
     rates = {
         (n, j): jnp.broadcast_to(rate_v[pl.ds(mine_at(shifts[n]) * halves + j, 1), :], (SEGS, LANES))
-        for n, j in away + home
+        for n, j in home
     }
-    prod = {at: ones for at in away + home}
+    prod = {at: ones for at in home}
     for i in range(steps):
-        for at in away + home:
+        for at in home:
             d = dec_v[at[0], at[1], pl.ds(i, SEGS, stride=steps), :]
             prod[at] = d * prod[at]
             dm[at[0], at[1], i] = d
             pm[at[0], at[1], i] = prod[at]
-    back = {at: ones for at in away + home}
-    linear = {at: zeros for at in away + home}
+    back = {at: ones for at in home}
+    linear = {at: zeros for at in home}
     for i in reversed(range(steps)):
-        for at in away + home:
+        for at in home:
             n, j = at
             g = sg_v[n, j, pl.ds(i, SEGS, stride=steps), :]
             if i == steps - 1:
@@ -206,7 +206,7 @@
                 qm[j, i] = back[at]
                 bm[j, i] = linear[at]
     p_levels, q_levels, p_before, q_after, b_after = {}, {}, {}, {}, {}
-    for at in away + home:
+    for at in home:
         p_levels[at], p_all = factor_levels(prod[at], 1)
         q_levels[at], q_all = factor_levels(back[at], -1)
         p_before[at] = shift_rows(p_all, 1, 1.0)
@@ -221,40 +221,6 @@
     if last > 0:
         hand_over(last, total)
 
-    def summaries(group):
-        state = {at: zeros for at in group}
-        for i in range(steps):
-            for at in group:
-                n, j = at
-                inflow = acc[n, j, pl.ds(i, SEGS, stride=steps), :]
-                if n == last:
-                    um[j, i] = inflow
-                state[at] = dm[n, j, i] * state[at] + inflow
-                fm[n, j, i] = state[at]
-        back = {at: zeros for at in group}
-        for i in reversed(range(steps)):
-            for at in group:
-                n, j = at
-                back[at] = gm[n, j, i] * back[at] + cm[n, j, i] * fm[n, j, i]
-        result = {}
-        for at in group:
-            f_all = chain_rows(p_levels[at], state[at], 1)
-            f_before = shift_rows(f_all, 1, 0.0)
-            a_all = chain_rows(q_levels[at], back[at] + linear[at] * f_before, -1)
-            result[at] = (f_all[SEGS - 1:SEGS], a_all[0:1])
-        return result
-
-    part_copies = []
-    away_result = summaries(away)
-    for n in range(last):
-        for j in range(halves):
-            part_send[n, j, 0:1], part_send[n, j, 1:2] = away_result[n, j]
-        copy = pltpu.make_async_remote_copy(
-            part_send.at[n], part_recv.at[n], ps_sem.at[n], pr_sem.at[n],
-            device_id=(tm, mine_at(shifts[n])), device_id_type=MESH,
-        )
-        copy.start()
-        part_copies.append(copy)
     early_copies = []
     for k in range(1, nt):
         copy = pltpu.make_async_remote_copy(
@@ -266,24 +232,7 @@
 
     for at in home:
         join(*at)
-    home_result = summaries(home)
-    for copy in part_copies:
-        copy.wait_recv()
-    for n, j in home:
-        f_row, a_row = home_result[n, j]
-        for source in range(last):
-            f_row = f_row + part_recv[source, j, 0:1]
-            a_row = a_row + part_recv[source, j, 1:2]
-        late[tm, j, 0:1] = f_row
-        late[tm, j, 1:2] = a_row
     late_copies = []
-    for k in range(1, nt):
-        copy = pltpu.make_async_remote_copy(
-            late.at[tm], late.at[tm], ls_sem.at[k], lr_sem.at[k],
-            device_id=(lax.rem(tm + k, nt), sensor), device_id_type=MESH,
-        )
-        copy.start()
-        late_copies.append(copy)
     f_before, a_after = {}, {}
     for at in home:
         j = at[1]
@@ -291,7 +240,7 @@
             y_copies[n, j].wait_recv()
         state = zeros
         for i in range(steps):
-            inflow = um[j, i]
+            inflow = acc[last, j, pl.ds(i, SEGS, stride=steps), :]
             for n in range(last):
                 inflow = inflow + yrecv[n, j, pl.ds(i, SEGS, stride=steps), :]
             state = dm[last, j, i] * state + inflow
@@ -300,14 +249,26 @@
         for i in reversed(range(steps)):
             back = gm[last, j, i] * back + cm[last, j, i] * fm[last, j, i]
             am[j, i] = back
-        f_before[at] = shift_rows(chain_rows(p_levels[at], state, 1), 1, 0.0)
+        f_all = chain_rows(p_levels[at], state, 1)
+        f_before[at] = shift_rows(f_all, 1, 0.0)
         a_all = chain_rows(q_levels[at], back + linear[at] * f_before[at], -1)
         a_after[at] = shift_rows(a_all, -1, 0.0)
-
-    for copy in early_copies + late_copies:
+        late[tm, j, 0:1] = f_all[SEGS - 1:SEGS]
+        late[tm, j, 1:2] = a_all[0:1]
+        for k in range(1, nt):
+            copy = pltpu.make_async_remote_copy(
+                late.at[tm, j], late.at[tm, j], ls_sem.at[j, k], lr_sem.at[j, k],
+                device_id=(lax.rem(tm + k, nt), sensor), device_id_type=MESH,
+            )
+            copy.start()
+            late_copies.append(copy)
+
+    for copy in early_copies:
         copy.wait_recv()
     for at in home:
         j = at[1]
+        for copy in late_copies[j * (nt - 1):(j + 1) * (nt - 1)]:
+            copy.wait_recv()
         entry = first_v[pl.ds(sensor * halves + j, 1), :]
         entries, mine = [], entry
         for t in range(nt):
@@ -330,7 +291,7 @@
 
     for copy in list(core_copies.values()) + list(y_copies.values()):
         copy.wait_send()
-    for copy in part_copies + early_copies + late_copies:
+    for copy in early_copies + late_copies:
         copy.wait_send()
 
 
@@ -362,15 +323,13 @@
             pltpu.VMEM((ny, depth, 2 * width), jnp.bfloat16),
             planes, planes, params, params,
             pltpu.VMEM((ny, 2, halves, hours, LANES), f32), planes, planes, planes,
-            tiles, group_tiles, tiles, group_tiles, group_tiles, group_tiles, group_tiles, tiles, tiles,
+            group_tiles, tiles, group_tiles, group_tiles, group_tiles, group_tiles, tiles, tiles,
             pltpu.VMEM((nt, halves, 4, LANES), f32),
             pltpu.VMEM((nt, halves, 2, LANES), f32),
-            pltpu.VMEM((ny, halves, 2, LANES), f32),
-            pltpu.VMEM((ny, halves, 2, LANES), f32),
             plane, plane,
             dma((CHUNKS,)), dma((CHUNKS,)), dma((ny,)), dma, dma((ny, halves)), dma((ny, halves)), dma((2,)),
             dma((ny, halves)), dma((ny, halves)), dma((ny, halves)), dma((ny, halves)),
-            dma((ny,)), dma((ny,)), dma((nt,)), dma((nt,)), dma((nt,)), dma((nt,)),
+            dma((nt,)), dma((nt,)), dma((halves, nt)), dma((halves, nt)),
         ],
         compiler_params=pltpu.CompilerParams(
             collective_id=0, has_side_effects=True, vmem_limit_bytes=56 * 1024 * 1024

time: 24.2 us -> 24.3 us (level)
  no operation moved by 1% of the time
where the time goes in v8:
time: 24.3 us; the launch traced here: 24.1 us
  Pallas kernels  22.1 us (91%)
  local copies, waits for them, and re-layouts  1.41 us (6%)
  between operations  0.64 us (3%)
    pallas_call x1, Pallas kernels, per_device(): pl.pallas_call(functools.partial(kernel, nt, ny), out_shape=(out, out), i...  22.1 us
    unnamed x2, local copies, waits for them, and re-layouts  1.41 us

profile of v8, /device:TPU:0, one launch (start us, length us, event | category | flops | bytes accessed | tf_op | source)
XLA Modules:
  0.0 24.1 jit_solution(14071849040111647943)
XLA Ops:
  0.6 22.1 %shard_map.86 = (f32[256,256]{1,0:T(8,128)S(1)}, f32[256,256]{1,0:T(8,128)S(1)}) custom-call(bf16[256,4096]{1,0:T(8,128)(2,1)} %obs.1, s32[16,256]{1,0:T(8,128)} %bitcast.3, bf16[4096,1024]{1,0:T(8,128)(2,1)} %gain.1, f32[256,1024]{1,0:T(8,128)} %decay.1, f32[256,1024]{1,0:T(8,128)} %sgain.1, f32[8,128]{1,0:T(8,128)} %bitcast.4, f32[8,128]{1,0:T(8,128)} %bitcast.5), custom_call_target="tpu_custom_call" | custom-call | flops 2147483648 | bytes 10485760 | tf_op jit(solution)/shard_map/pallas_call | solution.py:315
  22.7 0.7 %copy.11 = f32[256,256]{1,0:T(8,128)} copy(f32[256,256]{1,0:T(8,128)S(1)} %get-tuple-element.2) | data formatting | bytes 524288
  23.4 0.7 %copy.12 = f32[256,256]{1,0:T(8,128)} copy(f32[256,256]{1,0:T(8,128)S(1)} %get-tuple-element.3) | data formatting | bytes 524288
